TPU v7x, 32 devices: a whole 2x2x4 slice. The times are simulated.
32 devices in a mesh: section: 16 (over z, y, x), attn: 2 (over core).
Axes of the slice: x: 2, y: 2, z: 4, core: 2. Of those that a mesh axis runs over, the one named last changes fastest.
Arguments:
- queries: bfloat16 [8192, 3072], P(('section', 'attn')), may hold values from -120 to 120
- keys: bfloat16 [8192, 1024], P(('section', 'attn')), may hold values from -2.5 to 2.5
- values: bfloat16 [8192, 1024], P(('section', 'attn')), may hold values from -4 to 4
- doc_ids: int32 [8192], replicated, may hold values from 0 to 15, never falling along the last dimension, each value on 1 to 1792 neighbouring positions
Outputs:
- attended: bfloat16 [8192, 3072], P(('section', 'attn'))
Inputs may be any that keep to these rules, and one draw needn't show every extreme that they name: `doc_ids`: along the pack the document numbers never fall, and a document holds at most 1792 tokens.
All inputs are finite; a program needn't handle non-finite values.
Results may differ from a plain program's by a relative error of at most 0.0028.
Values may be sent and summed in bfloat16 or wider, within the bound.
No kernel may reach another device: no remote copies, remote signals or barrier semaphores. Data moves between devices by JAX's collectives and lax.ppermute only.
A program may use at most 64 MiB of HBM per device.

v0:
```python
import functools
import math

import jax
import jax.numpy as jnp
from jax import lax
from jax.experimental import pallas as pl
from jax.experimental.pallas import tpu as pltpu
from jax.sharding import PartitionSpec as P

HEAD_DIM = 128
REACH = 8
AXES = ("section", "attn")
NEG = -1e30
SCALE = HEAD_DIM ** -0.5 * math.log2(math.e)
HEADS_STEP = 4
VMEM_BYTES = 16 * 2**20
HIGH = 2.0 ** 60
barrier = lax.optimization_barrier


def scores(q, k):
    return lax.dot_general(q, k, (((1,), (1,)), ((), ())), preferred_element_type=jnp.float32)


def heads_of(ref, step, count):
    at = pl.multiple_of(step * (count * HEAD_DIM), HEAD_DIM)
    return [ref[:, pl.ds(at + i * HEAD_DIM, HEAD_DIM)] for i in range(count)]


def put_head(ref, step, count, i, value):
    at = pl.multiple_of(step * (count * HEAD_DIM), HEAD_DIM)
    ref[:, pl.ds(at + i * HEAD_DIM, HEAD_DIM)] = value


def with_ones(v, ok):
    return jnp.concatenate([v * ok, ok], axis=1)


def where_am_i(ids, docs_ref, rows):
    chip, core = ids[0], ids[1]
    first = (chip * ids[2] + core) * rows
    head = docs_ref[pl.ds(first // HEAD_DIM, 1), :][:, :1]
    earlier = (docs_ref[...] < head).astype(jnp.int32)
    return chip, core, first, jnp.sum(earlier), head


def own_kernel(group, ids, docs_ref, q_ref, k_ref, v_ref, acc_ref, top_ref, total_ref):
    rows = q_ref.shape[0]
    count = HEADS_STEP * group
    _, _, first, _, head = where_am_i(ids, docs_ref, rows)
    tiles = [docs_ref[pl.ds(first // HEAD_DIM + i, 1), :] for i in range(rows // HEAD_DIM)]
    across = jnp.concatenate(tiles, axis=1)
    down = jnp.concatenate([jnp.broadcast_to(t, (HEAD_DIM, HEAD_DIM)).T for t in tiles], axis=0)
    same = jnp.concatenate([down] * (rows // HEAD_DIM), axis=1) == across
    at = lax.broadcasted_iota(jnp.int32, (rows, rows), 1)
    row = lax.broadcasted_iota(jnp.int32, (rows, rows), 0)
    bias = jnp.where(same & (at <= row), 0.0, NEG)
    sees_earlier = down == head

    def step(j, _):
        qs = heads_of(q_ref, j, count)
        ks, vs = heads_of(k_ref, j, HEADS_STEP), heads_of(v_ref, j, HEADS_STEP)
        for i in range(count):
            s = scores(qs[i], ks[i // group]) + bias
            top = jnp.max(s, axis=1, keepdims=True)
            w = jnp.exp2((s - top) * SCALE).astype(jnp.bfloat16)
            v = vs[i // group]
            both = jnp.dot(w, with_ones(v, jnp.ones_like(v)), preferred_element_type=jnp.float32)
            put_head(acc_ref, j, count, i, both[:, :HEAD_DIM])
            total_ref[j * count + i] = both[:, HEAD_DIM:]
            top_ref[j * count + i] = jnp.where(sees_earlier, jnp.broadcast_to(top, (rows, HEAD_DIM)), -NEG)
        return 0

    lax.fori_loop(0, k_ref.shape[1] // HEAD_DIM // HEADS_STEP, step, 0)


def far_kernel(choose, devices, last, group, ids, docs_ref, q_ref, acc_in, top_in, total_in, *refs):
    rows = q_ref.shape[0]
    chip, core, first, start, _ = where_am_i(ids, docs_ref, rows)
    plane, owner = chip % 4, first // rows
    places = [jnp.where((d >= 0) & (d < owner), d * rows, -(2**30)) for d in devices(plane, core, chip * ids[2])]
    if last:
        refs, (hbm, acc_out, sems) = refs[:-3], refs[-3:]
    else:
        refs, (acc_out, top_out, total_out) = refs[:-3], refs[-3:]
    count = HEADS_STEP * group
    steps = refs[0].shape[1] // HEAD_DIM // HEADS_STEP
    needed = functools.reduce(jnp.maximum, places) + rows > start

    def put(j, i, total, out, top=None):
        if last:
            out = (out / total).astype(jnp.bfloat16)
        else:
            if top is not None:
                top_out[j * count + i] = top
            total_out[j * count + i] = total
        put_head(acc_out, j, count, i, out)

    def attend(j, exact):
        qs, befores = heads_of(q_ref, j, count), heads_of(acc_in, j, count)
        tiles = [heads_of(r, j, HEADS_STEP) for r in refs]
        at = lax.broadcasted_iota(jnp.int32, (rows, HEAD_DIM), 0)
        high = None
        for h in range(HEADS_STEP):
            ks, vs = choose(plane, core, [t[h] for t in tiles])
            k = jnp.concatenate(ks, axis=0)
            ok = [jnp.where(at + place >= start, 1.0, 0.0).astype(jnp.bfloat16) for place in places]
            v = jnp.concatenate([with_ones(v, o) for v, o in zip(vs, ok)], axis=0)
            for i in range(h * group, (h + 1) * group):
                s = scores(qs[i], k)
                top, total, before = top_in[j * count + i], total_in[j * count + i], befores[i]
                if exact:
                    key = lax.broadcasted_iota(jnp.int32, (rows, rows), 1)
                    allowed = jnp.concatenate([key + place >= start for place in places], axis=1)
                    s = jnp.where(allowed, s, NEG)
                    new = jnp.maximum(top, jnp.max(s, axis=1, keepdims=True))
                    back = jnp.exp2((top - new) * SCALE)
                    top, total, before = new, total * back, before * back
                w = []
                for n in range(k.shape[0] // HEAD_DIM):
                    part = jnp.exp2((s[:, n * HEAD_DIM:(n + 1) * HEAD_DIM] - top) * SCALE).astype(jnp.bfloat16)
                    w.append(part)
                    if not exact:
                        high = part if high is None else jnp.maximum(high, part)
                both = jnp.dot(jnp.concatenate(w, axis=1), v, preferred_element_type=jnp.float32)
                put(j, i, total + both[:, HEAD_DIM:], both[:, :HEAD_DIM] + before, top if exact else None)
        return high

    def step(j, _):
        @pl.when(needed)
        def _():
            high = attend(j, False)

            @pl.when(jnp.max(high.astype(jnp.float32)) > HIGH)
            def _():
                attend(j, True)

        @pl.when(jnp.logical_not(needed))
        def _():
            for i, before in enumerate(heads_of(acc_in, j, count)):
                put(j, i, total_in[j * count + i], before)

        if last:
            part(j).start()
        return 0

    def part(j):
        width = count * HEAD_DIM
        columns = pl.ds(pl.multiple_of(j * width, width), width)
        return pltpu.make_async_copy(acc_out.at[:, columns], hbm.at[:, columns], sems.at[j])

    lax.fori_loop(0, steps, step, 0)
    if last:
        for j in range(steps):
            part(j).wait()


def pick(plane, at0, at1, at2, at3):
    return jnp.where(plane == 0, at0, jnp.where(plane == 1, at1, jnp.where(plane == 2, at2, at3)))


def choose_first(plane, core, tiles):
    return tiles[:1], tiles[1:]


def devices_first(plane, core, base):
    return (jnp.where(core == 1, base, jnp.where(plane == 0, base - 7, -1)),)


def choose_middle(plane, core, tiles):
    x1, y1, x2, y2, z2 = tiles
    pk, pv = pick(plane, x2, x2, y2, x2), pick(plane, z2, x1, y1, x1)
    qk, qv = pick(plane, y2, y2, x2, y2), pick(plane, z2, z2, z2, y1)
    return (pk, qk), (pv, qv)


def devices_middle(mates, plane, core, base):
    part = 1 - core if mates else core
    return base - 2 * pick(plane, 3, 1, 2, 1) + part, pick(plane, -8, base - 4, base - 6, base - 4) + part


def choose_last(plane, core, tiles):
    z1, y2, x3, y3, z3 = tiles
    pk, pv = pick(plane, y2, x3, x3, x3), pick(plane, z3, y3, y3, y3)
    qk, qv = pick(plane, x3, z1, z1, z1), pick(plane, y3, z3, z3, z3)
    return (pk, qk), (pv, qv)


def devices_last(mates, plane, core, base):
    part = 1 - core if mates else core
    return base - 2 * pick(plane, 2, 3, 1, 3) + part, base - 2 * pick(plane, 1, 4, 4, 4) + part


def call(kernel, ids, docs, q, carry, pieces, keys, last=False):
    rows, width = q.shape
    steps = pieces[0].shape[1] // HEAD_DIM // HEADS_STEP
    group = width // pieces[0].shape[1]
    vmem = pl.BlockSpec(memory_space=pltpu.VMEM)
    arrays = [docs, q, *carry, *pieces]
    if last:
        out_shape = [jax.ShapeDtypeStruct(q.shape, jnp.bfloat16)]
        scratch = [pltpu.VMEM(q.shape, jnp.bfloat16), pltpu.SemaphoreType.DMA((steps,))]
    else:
        out_shape = [jax.ShapeDtypeStruct(q.shape, jnp.float32)]
        out_shape += [jax.ShapeDtypeStruct((width // HEAD_DIM, rows, HEAD_DIM), jnp.float32)] * 2
        scratch = []
    return pl.pallas_call(
        functools.partial(kernel, group),
        in_specs=[pl.BlockSpec(memory_space=pltpu.SMEM)] + [vmem] * len(arrays),
        out_specs=[pl.BlockSpec(memory_space=pl.ANY) if last else vmem] * len(out_shape),
        out_shape=out_shape,
        scratch_shapes=scratch,
        input_output_aliases={4: 1} if carry and not last else {},
        cost_estimate=pl.CostEstimate(
            flops=8 * rows * keys * width, bytes_accessed=4 * rows * width, transcendentals=0
        ),
        compiler_params=pltpu.CompilerParams(vmem_limit_bytes=VMEM_BYTES),
    )(ids, *arrays)


def shards(queries, keys, values, doc_ids):
    rows = queries.shape[0]
    chips, cores = lax.axis_size("section"), lax.axis_size("attn")
    chip, core = lax.axis_index("section"), lax.axis_index("attn")
    plane, odd_x, odd_y = chip % 4, chip % 2, (chip // 2) % 2

    def routes(target):
        return [
            (c * cores + k, at * cores + to)
            for c in range(chips) for k in range(cores) for at, to in [target(c, k)]
        ]

    along = {
        "x": routes(lambda c, k: (c ^ 1, k)),
        "y": routes(lambda c, k: (c ^ 2, k)),
        "z": routes(lambda c, k: ((c + 4) % chips, k)),
        "mate": routes(lambda c, k: (c, 1 - k)),
        "first_z": routes(lambda c, k: ((c + 4) % chips, k) if c % 4 else (c, 1 - k)),
        "first_mate": routes(lambda c, k: ((c + 4) % chips, 0) if c % 4 == 0 and k else (c, 1 - k)),
    }

    def send(array, way):
        return lax.ppermute(array, AXES, along[way])

    def swap(*arrays):
        return tuple(send(a, "mate") for a in arrays)

    ids = jnp.stack([chip, core, jnp.int32(cores)])
    docs = doc_ids.reshape(-1, HEAD_DIM)
    w = jnp.where

    def far(choose, devices, carry, pieces, keys, last=False):
        kernel = functools.partial(far_kernel, choose, devices, last)
        return call(kernel, ids, docs, queries, carry, pieces, keys, last)

    z1 = send(keys, "first_z")
    x1, y1 = send(values, "x"), send(values, "y")
    mate_k, mate_v = send(keys, "first_mate"), send(values, "first_mate")
    z1, mate_k, mate_v = barrier((z1, mate_k, mate_v))
    across2, side2 = w(odd_x == 0, keys, z1), w(odd_y == 0, keys, z1)
    x2, y2 = send(across2, "x"), send(side2, "y")
    x1, y1, _, _ = barrier((x1, y1, across2, side2))
    z2 = send(w(plane == 1, y1, x1), "z")
    x1s, y1s = swap(x1, y1)
    carry = call(own_kernel, ids, docs, queries, (), [keys, values], rows)
    carry = far(choose_first, devices_first, carry, [mate_k, mate_v], rows)
    y2, z2, y1, x1s, y1s, *carry = barrier((y2, z2, y1, x1s, y1s, *carry))
    x3 = send(y2, "x")
    side3, up3 = w(odd_y == 0, x1, z2), w(plane == 0, y1, values)
    y3, z3 = send(side3, "y"), send(up3, "z")
    x2s, y2s, z2s = swap(x2, y2, z2)
    carry = far(choose_middle, functools.partial(devices_middle, False), carry, [x1, y1, x2, y2, z2], 2 * rows)
    x2s, y2s, z2s, *carry = barrier((x2s, y2s, z2s, *carry))
    carry = far(choose_middle, functools.partial(devices_middle, True), carry, [x1s, y1s, x2s, y2s, z2s], 2 * rows)
    x3, y3, z3, *carry = barrier((x3, y3, z3, *carry))
    z1s, x3s, y3s, z3s = swap(z1, x3, y3, z3)
    carry = far(choose_last, functools.partial(devices_last, False), carry, [z1, y2, x3, y3, z3], 2 * rows)
    (out,) = far(
        choose_last, functools.partial(devices_last, True), carry, [z1s, y2s, x3s, y3s, z3s], 2 * rows, True
    )
    return out


def solution(mesh):
    split = P(AXES, None)
    return jax.shard_map(
        shards, mesh=mesh, in_specs=(split, split, split, P()), out_specs=split, check_vma=False
    )
```

profile of v0, /device:TPU:4, one launch (start us, length us, event | category | flops | bytes accessed | tf_op | source)
XLA Modules:
  0.0 65.4 jit_solution(13877009297684617747)
XLA Ops:
  0.0 0.0 copy-start.3
  0.0 0.0 copy-start
  0.0 1.6 %collective-permute-start = (bf16[256,1024]{1,0:T(8,128)(2,1)}, bf16[256,1024]{1,0:T(8,128)(2,1)S(1)}, u32[]{:S(2)}, u32[]{:S(2)}) collective-permute-start(bf16[256,1024]{1,0:T(8,128)(2,1)} %k_ref.1), channel_id=1, source_target_pairs={{0,1},{1,0},{2,10},{3,11},{4,12},{5,13},{6,14},{7,15},{8,9},{9,8},... | collective-permute-start | bytes 1572872 | tf_op jit(solution)/shard_map/ppermute | solution.py:244
  1.6 0.0 collective-permute-start.1
  1.6 0.5 collective-permute-start.2
  2.1 1.5 %collective-permute-start.4 = (bf16[256,1024]{1,0:T(8,128)(2,1)}, bf16[256,1024]{1,0:T(8,128)(2,1)S(1)}, u32[]{:S(2)}, u32[]{:S(2)}) collective-permute-start(bf16[256,1024]{1,0:T(8,128)(2,1)} %v_ref.1), channel_id=1, source_target_pairs={{0,2},{1,3},{2,0},{3,1},{4,6},{5,7},{6,4},{7,5},{8,10},{9,11},{10,... | collective-permute-start | bytes 1572872 | tf_op jit(solution)/shard_map/ppermute | solution.py:244
  3.6 0.5 collective-permute-start.5
  4.1 11.6 %collective-permute-done.refs_0_ = bf16[256,1024]{1,0:T(8,128)(2,1)S(1)} collective-permute-done((bf16[256,1024]{1,0:T(8,128)(2,1)}, bf16[256,1024]{1,0:T(8,128)(2,1)S(1)}, u32[]{:S(2)}, u32[]{:S(2)}) %collective-permute-start) | collective-permute-done | bytes 524320 | tf_op jit(solution)/shard_map/ppermute | solution.py:244
  15.7 0.0 copy-start.1
  15.7 0.0 collective-permute-done.1.refs_0_
  15.7 0.0 collective-permute-done.2.refs_1_
  15.7 2.3 %broadcast_select_fusion.1 = (bf16[256,1024]{1,0:T(8,128)(2,1)}, bf16[256,1024]{1,0:T(8,128)(2,1)}) fusion(bf16[256,1024]{1,0:T(8,128)(2,1)} %k_ref.1, bf16[256,1024]{1,0:T(8,128)(2,1)S(1)} %collective-permute-done.refs_0_, pred[]{:T(512)S(6)} %eq.19, pred[]{:T(512)S(6)} %eq.17), kind=kLoop, calls=%fused_computation.1 | loop fusion | flops 524288 | bytes 2097154 | tf_op jit(solution)/shard_map/jit(_where)/select_n | solution.py:261
  18.0 0.0 collective-permute-done.4.refs_0_
  18.0 0.0 collective-permute-done.5.refs_1_
  18.0 0.0 copy-done.1
  18.0 0.8 %broadcast_select_fusion.2 = bf16[256,1024]{1,0:T(8,128)(2,1)} fusion(bf16[256,1024]{1,0:T(8,128)(2,1)S(1)} %collective-permute-done.5.refs_1_, bf16[256,1024]{1,0:T(8,128)(2,1)S(1)} %collective-permute-done.4.refs_0_, pred[]{:T(512)S(6)} %eq.18), kind=kLoop, calls=%fused_computation.2 | loop fusion | flops 262144 | bytes 1572865 | tf_op jit(solution)/shard_map/jit(_where)/select_n | solution.py:264
  18.9 0.9 %collective-permute-start.6 = (bf16[256,1024]{1,0:T(8,128)(2,1)}, bf16[256,1024]{1,0:T(8,128)(2,1)S(1)}, u32[]{:S(2)}, u32[]{:S(2)}) collective-permute-start(bf16[256,1024]{1,0:T(8,128)(2,1)} %broadcast_select_fusion.2), channel_id=1, source_target_pairs={{0,8},{1,9},{2,10},{3,11},{4,12},{5,13},{6,14},{7,15},{8,16},{9,17... | collective-permute-start | bytes 1572872 | tf_op jit(solution)/shard_map/ppermute | solution.py:244
  19.8 0.0 collective-permute-start.7
  19.8 0.5 collective-permute-start.8
  20.3 0.5 collective-permute-start.3
  20.8 0.1 pad_add_fusion.ids
  20.9 0.6 collective-permute-start.12
  21.5 0.0 copy-done.3
  21.5 0.0 copy-done
  21.5 0.0 copy-start.4
  21.5 1.0 %copy-done.4 = bf16[256,1024]{1,0:T(8,128)(2,1)S(1)} copy-done((bf16[256,1024]{1,0:T(8,128)(2,1)S(1)}, bf16[256,1024]{1,0:T(8,128)(2,1)}, u32[]{:S(2)}) %copy-start.4) | copy-done | bytes 524312
  22.6 1.0 %copy-done.6 = bf16[256,1024]{1,0:T(8,128)(2,1)S(1)} copy-done((bf16[256,1024]{1,0:T(8,128)(2,1)S(1)}, bf16[256,1024]{1,0:T(8,128)(2,1)}, u32[]{:S(2)}) %copy-start.6) | copy-done | bytes 524312
  23.6 3.1 %shard_map.46 = (f32[256,3072]{1,0:T(8,128)S(1)}, f32[24,256,128]{2,1,0:T(8,128)S(1)}, f32[24,256,128]{2,1,0:T(8,128)S(1)}) custom-call(s32[3]{0:T(128)S(1)} %pad_add_fusion.ids, s32[64,128]{1,0:T(8,128)S(1)} %bitcast.3, bf16[256,3072]{1,0:T(8,128)(2,1)S(1)} %copy-done, bf16[256,1024]{1,0:T(8,128)(2,1)S(1)} %copy-done.6, bf16[256,1024]{1,0:T(8,128)(2,1)S(1)} %copy-done.4), custom_call_target="tpu_custom_call" | custom-call | flops 1610612736 | bytes 3145728 | tf_op jit(solution)/shard_map/pallas_call | solution.py:208
  26.7 0.0 copy-start.5
  26.7 2.3 %shard_map.47 = (f32[256,3072]{1,0:T(8,128)S(1)}, f32[24,256,128]{2,1,0:T(8,128)S(1)}, f32[24,256,128]{2,1,0:T(8,128)S(1)}) custom-call(s32[3]{0:T(128)S(1)} %pad_add_fusion.ids, s32[64,128]{1,0:T(8,128)S(1)} %bitcast.4, bf16[256,3072]{1,0:T(8,128)(2,1)S(1)} %copy-done, f32[256,3072]{1,0:T(8,128)S(1)} %get-tuple-element.48.acc_in, ...), custom_call_target="tpu_custom_call", output_to_operand_aliasing={{1}: (4, {})} | custom-call | flops 1610612736 | bytes 3145728 | tf_op jit(solution)/shard_map/pallas_call | solution.py:208
  29.0 4.7 %collective-permute-done.6.refs_4_ = bf16[256,1024]{1,0:T(8,128)(2,1)S(1)} collective-permute-done((bf16[256,1024]{1,0:T(8,128)(2,1)}, bf16[256,1024]{1,0:T(8,128)(2,1)S(1)}, u32[]{:S(2)}, u32[]{:S(2)}) %collective-permute-start.6) | collective-permute-done | bytes 524320 | tf_op jit(solution)/shard_map/ppermute | solution.py:244
  33.8 0.0 collective-permute-done.7.refs_0_
  33.8 0.0 collective-permute-done.8.refs_1_
  33.8 0.7 %collective-permute-done.3.refs_3_.refs_1_ = bf16[256,1024]{1,0:T(8,128)(2,1)} collective-permute-done((bf16[256,1024]{1,0:T(8,128)(2,1)}, bf16[256,1024]{1,0:T(8,128)(2,1)}, u32[]{:S(2)}, u32[]{:S(2)}) %collective-permute-start.3) | collective-permute-done | bytes 524320 | tf_op jit(solution)/shard_map/ppermute | solution.py:244
  34.4 0.0 collective-permute-start.14
  34.4 1.0 %collective-permute-start.9 = (bf16[256,1024]{1,0:T(8,128)(2,1)}, bf16[256,1024]{1,0:T(8,128)(2,1)S(1)}, u32[]{:S(2)}, u32[]{:S(2)}) collective-permute-start(bf16[256,1024]{1,0:T(8,128)(2,1)} %collective-permute-done.3.refs_3_.refs_1_), channel_id=1, source_target_pairs={{0,2},{1,3},{2,0},{3,1},{4,6},{5,7},{6,4},{7,5},{8,10},{9,11},{10,... | collective-permute-start | bytes 1572872 | tf_op jit(solution)/shard_map/ppermute | solution.py:244
  35.4 0.2 collective-permute-start.15
  35.6 0.1 broadcast_select_fusion.3
  35.6 0.6 collective-permute-start.10
  36.2 0.0 collective-permute-done.12.refs_2_
  36.2 0.1 collective-permute-start.13
  36.3 0.0 copy-done.5
  36.3 0.1 broadcast_select_fusion
  36.3 0.0 copy-start.2
  36.4 0.2 collective-permute-done.14.refs_3_.refs_1_
  36.6 1.6 %collective-permute-start.11 = (bf16[256,1024]{1,0:T(8,128)(2,1)S(1)}, bf16[256,1024]{1,0:T(8,128)(2,1)S(1)}, u32[]{:S(2)}, u32[]{:S(2)}) collective-permute-start(bf16[256,1024]{1,0:T(8,128)(2,1)S(1)} %broadcast_select_fusion), channel_id=1, source_target_pairs={{0,8},{1,9},{2,10},{3,11},{4,12},{5,13},{6,14},{7,15},{8,16},{9,17... | collective-permute-start | bytes 1572872 | tf_op jit(solution)/shard_map/ppermute | solution.py:244
  38.1 2.1 %shard_map.48 = (f32[256,3072]{1,0:T(8,128)S(1)}, f32[24,256,128]{2,1,0:T(8,128)S(1)}, f32[24,256,128]{2,1,0:T(8,128)S(1)}) custom-call(s32[3]{0:T(128)S(1)} %pad_add_fusion.ids, s32[64,128]{1,0:T(8,128)S(1)} %bitcast.5, bf16[256,3072]{1,0:T(8,128)(2,1)S(1)} %copy-done, f32[256,3072]{1,0:T(8,128)S(1)} %get-tuple-element.59.acc_in, ...), custom_call_target="tpu_custom_call", output_to_operand_aliasing={{1}: (4, {})} | custom-call | flops 3221225472 | bytes 3145728 | tf_op jit(solution)/shard_map/pallas_call | solution.py:208
  40.2 0.0 collective-permute-done.15.refs_4_
  40.2 0.0 copy-done.2
  40.2 0.1 collective-permute-start.16
  40.3 0.0 collective-permute-done.13.refs_2_
  40.3 2.3 %shard_map.49 = (f32[256,3072]{1,0:T(8,128)S(1)}, f32[24,256,128]{2,1,0:T(8,128)S(1)}, f32[24,256,128]{2,1,0:T(8,128)S(1)}) custom-call(s32[3]{0:T(128)S(1)} %pad_add_fusion.ids, s32[64,128]{1,0:T(8,128)S(1)} %bitcast.6, bf16[256,3072]{1,0:T(8,128)(2,1)S(1)} %copy-done, f32[256,3072]{1,0:T(8,128)S(1)} %get-tuple-element.65.acc_in, ...), custom_call_target="tpu_custom_call", output_to_operand_aliasing={{1}: (4, {})} | custom-call | flops 3221225472 | bytes 3145728 | tf_op jit(solution)/shard_map/pallas_call | solution.py:208
  42.6 7.3 %collective-permute-done.10.refs_3_ = bf16[256,1024]{1,0:T(8,128)(2,1)S(1)} collective-permute-done((bf16[256,1024]{1,0:T(8,128)(2,1)S(1)}, bf16[256,1024]{1,0:T(8,128)(2,1)S(1)}, u32[]{:S(2)}, u32[]{:S(2)}) %collective-permute-start.10) | collective-permute-done | bytes 524320 | tf_op jit(solution)/shard_map/ppermute | solution.py:244
  49.9 2.8 %collective-permute-done.11.refs_4_ = bf16[256,1024]{1,0:T(8,128)(2,1)S(1)} collective-permute-done((bf16[256,1024]{1,0:T(8,128)(2,1)S(1)}, bf16[256,1024]{1,0:T(8,128)(2,1)S(1)}, u32[]{:S(2)}, u32[]{:S(2)}) %collective-permute-start.11) | collective-permute-done | bytes 524320 | tf_op jit(solution)/shard_map/ppermute | solution.py:244
  52.7 0.0 collective-permute-done.9.refs_2_
  52.7 0.0 collective-permute-start.17
  52.7 0.5 collective-permute-start.18
  53.2 0.0 collective-permute-start.19
  53.2 5.9 %shard_map.50 = (f32[256,3072]{1,0:T(8,128)S(1)}, f32[24,256,128]{2,1,0:T(8,128)S(1)}, f32[24,256,128]{2,1,0:T(8,128)S(1)}) custom-call(s32[3]{0:T(128)S(1)} %pad_add_fusion.ids, s32[64,128]{1,0:T(8,128)S(1)} %bitcast.7, bf16[256,3072]{1,0:T(8,128)(2,1)S(1)} %copy-done, f32[256,3072]{1,0:T(8,128)S(1)} %get-tuple-element.76.acc_in, ...), custom_call_target="tpu_custom_call", output_to_operand_aliasing={{1}: (4, {})} | custom-call | flops 3221225472 | bytes 3145728 | tf_op jit(solution)/shard_map/pallas_call | solution.py:208
  59.1 0.0 collective-permute-done.16.refs_0_
  59.1 0.0 collective-permute-done.17.refs_2_
  59.1 0.0 collective-permute-done.18.refs_3_
  59.2 0.0 collective-permute-done.19.refs_4_
  59.2 6.0 %shard_map.51 = bf16[256,3072]{1,0:T(8,128)(2,1)} custom-call(s32[3]{0:T(128)S(1)} %pad_add_fusion.ids, s32[64,128]{1,0:T(8,128)S(1)} %bitcast.8, bf16[256,3072]{1,0:T(8,128)(2,1)S(1)} %copy-done, f32[256,3072]{1,0:T(8,128)S(1)} %get-tuple-element.82.acc_in, f32[24,256,128]{2,1,0:T(8,128)S(1)} %get-tuple-element.83.top_in, ...), custom_call_target="tpu_custom_call" | custom-call | flops 3221225472 | bytes 3145728 | tf_op jit(solution)/shard_map/pallas_call | solution.py:208
  (1 shorter events, 0.0 us)
Async XLA Ops:
  0.0 21.5 %copy-start.3 = (s32[8192]{0:T(1024)S(1)}, s32[8192]{0:T(1024)}, u32[]{:S(2)}) copy-start(s32[8192]{0:T(1024)} %param.7) | copy-start | bytes 98308
  0.0 21.5 %copy-start = (bf16[256,3072]{1,0:T(8,128)(2,1)S(1)}, bf16[256,3072]{1,0:T(8,128)(2,1)}, u32[]{:S(2)}) copy-start(bf16[256,3072]{1,0:T(8,128)(2,1)} %q_ref.11) | copy-start | bytes 4718596
  0.0 15.7 %collective-permute-start = (bf16[256,1024]{1,0:T(8,128)(2,1)}, bf16[256,1024]{1,0:T(8,128)(2,1)S(1)}, u32[]{:S(2)}, u32[]{:S(2)}) collective-permute-start(bf16[256,1024]{1,0:T(8,128)(2,1)} %k_ref.1), channel_id=1, source_target_pairs={{0,1},{1,0},{2,10},{3,11},{4,12},{5,13},{6,14},{7,15},{8,9},{9,8},... | collective-permute-start | bytes 1572872 | tf_op jit(solution)/shard_map/ppermute | solution.py:244
  1.6 14.2 %collective-permute-start.1 = (bf16[256,1024]{1,0:T(8,128)(2,1)}, bf16[256,1024]{1,0:T(8,128)(2,1)}, u32[]{:S(2)}, u32[]{:S(2)}) collective-permute-start(bf16[256,1024]{1,0:T(8,128)(2,1)} %k_ref.1), channel_id=1, source_target_pairs={{0,1},{1,8},{2,3},{3,2},{4,5},{5,4},{6,7},{7,6},{8,9},{9,16},{10,1... | collective-permute-start | bytes 1572872 | tf_op jit(solution)/shard_map/ppermute | solution.py:244
  1.6 14.2 %collective-permute-start.2 = (bf16[256,1024]{1,0:T(8,128)(2,1)}, bf16[256,1024]{1,0:T(8,128)(2,1)}, u32[]{:S(2)}, u32[]{:S(2)}) collective-permute-start(bf16[256,1024]{1,0:T(8,128)(2,1)} %v_ref.1), channel_id=1, source_target_pairs={{0,1},{1,8},{2,3},{3,2},{4,5},{5,4},{6,7},{7,6},{8,9},{9,16},{10,1... | collective-permute-start | bytes 1572872 | tf_op jit(solution)/shard_map/ppermute | solution.py:244
  2.1 15.9 %collective-permute-start.4 = (bf16[256,1024]{1,0:T(8,128)(2,1)}, bf16[256,1024]{1,0:T(8,128)(2,1)S(1)}, u32[]{:S(2)}, u32[]{:S(2)}) collective-permute-start(bf16[256,1024]{1,0:T(8,128)(2,1)} %v_ref.1), channel_id=1, source_target_pairs={{0,2},{1,3},{2,0},{3,1},{4,6},{5,7},{6,4},{7,5},{8,10},{9,11},{10,... | collective-permute-start | bytes 1572872 | tf_op jit(solution)/shard_map/ppermute | solution.py:244
  3.6 14.4 %collective-permute-start.5 = (bf16[256,1024]{1,0:T(8,128)(2,1)}, bf16[256,1024]{1,0:T(8,128)(2,1)S(1)}, u32[]{:S(2)}, u32[]{:S(2)}) collective-permute-start(bf16[256,1024]{1,0:T(8,128)(2,1)} %v_ref.1), channel_id=1, source_target_pairs={{0,4},{1,5},{2,6},{3,7},{4,0},{5,1},{6,2},{7,3},{8,12},{9,13},{10,... | collective-permute-start | bytes 1572872 | tf_op jit(solution)/shard_map/ppermute | solution.py:244
  15.7 2.3 %copy-start.1 = (bf16[256,1024]{1,0:T(8,128)(2,1)}, bf16[256,1024]{1,0:T(8,128)(2,1)S(1)}, u32[]{:S(2)}) copy-start(bf16[256,1024]{1,0:T(8,128)(2,1)S(1)} %collective-permute-done.refs_0_) | copy-start | bytes 1572868
  18.9 14.9 %collective-permute-start.6 = (bf16[256,1024]{1,0:T(8,128)(2,1)}, bf16[256,1024]{1,0:T(8,128)(2,1)S(1)}, u32[]{:S(2)}, u32[]{:S(2)}) collective-permute-start(bf16[256,1024]{1,0:T(8,128)(2,1)} %broadcast_select_fusion.2), channel_id=1, source_target_pairs={{0,8},{1,9},{2,10},{3,11},{4,12},{5,13},{6,14},{7,15},{8,16},{9,17... | collective-permute-start | bytes 1572872 | tf_op jit(solution)/shard_map/ppermute | solution.py:244
  19.8 14.0 %collective-permute-start.7 = (bf16[256,1024]{1,0:T(8,128)(2,1)S(1)}, bf16[256,1024]{1,0:T(8,128)(2,1)}, u32[]{:S(2)}, u32[]{:S(2)}) collective-permute-start(bf16[256,1024]{1,0:T(8,128)(2,1)S(1)} %collective-permute-done.4.refs_0_), channel_id=1, source_target_pairs={{0,1},{1,0},{2,3},{3,2},{4,5},{5,4},{6,7},{7,6},{8,9},{9,8},{10,11... | collective-permute-start | bytes 1572872 | tf_op jit(solution)/shard_map/ppermute | solution.py:244
  19.8 14.0 %collective-permute-start.8 = (bf16[256,1024]{1,0:T(8,128)(2,1)S(1)}, bf16[256,1024]{1,0:T(8,128)(2,1)}, u32[]{:S(2)}, u32[]{:S(2)}) collective-permute-start(bf16[256,1024]{1,0:T(8,128)(2,1)S(1)} %collective-permute-done.5.refs_1_), channel_id=1, source_target_pairs={{0,1},{1,0},{2,3},{3,2},{4,5},{5,4},{6,7},{7,6},{8,9},{9,8},{10,11... | collective-permute-start | bytes 1572872 | tf_op jit(solution)/shard_map/ppermute | solution.py:244
  20.3 14.1 %collective-permute-start.3 = (bf16[256,1024]{1,0:T(8,128)(2,1)}, bf16[256,1024]{1,0:T(8,128)(2,1)}, u32[]{:S(2)}, u32[]{:S(2)}) collective-permute-start(bf16[256,1024]{1,0:T(8,128)(2,1)} %get-tuple-element.86), channel_id=1, source_target_pairs={{0,4},{1,5},{2,6},{3,7},{4,0},{5,1},{6,2},{7,3},{8,12},{9,13},{10,... | collective-permute-start | bytes 1572872 | tf_op jit(solution)/shard_map/ppermute | solution.py:244
  20.9 15.3 %collective-permute-start.12 = (bf16[256,1024]{1,0:T(8,128)(2,1)}, bf16[256,1024]{1,0:T(8,128)(2,1)S(1)}, u32[]{:S(2)}, u32[]{:S(2)}) collective-permute-start(bf16[256,1024]{1,0:T(8,128)(2,1)} %get-tuple-element.85), channel_id=1, source_target_pairs={{0,2},{1,3},{2,0},{3,1},{4,6},{5,7},{6,4},{7,5},{8,10},{9,11},{10,... | collective-permute-start | bytes 1572872 | tf_op jit(solution)/shard_map/ppermute | solution.py:244
  21.5 1.0 %copy-start.4 = (bf16[256,1024]{1,0:T(8,128)(2,1)S(1)}, bf16[256,1024]{1,0:T(8,128)(2,1)}, u32[]{:S(2)}) copy-start(bf16[256,1024]{1,0:T(8,128)(2,1)} %v_ref.1) | copy-start | bytes 1572868
  22.6 1.0 %copy-start.6 = (bf16[256,1024]{1,0:T(8,128)(2,1)S(1)}, bf16[256,1024]{1,0:T(8,128)(2,1)}, u32[]{:S(2)}) copy-start(bf16[256,1024]{1,0:T(8,128)(2,1)} %k_ref.1) | copy-start | bytes 1572868
  26.7 9.6 %copy-start.5 = (bf16[256,1024]{1,0:T(8,128)(2,1)S(1)}, bf16[256,1024]{1,0:T(8,128)(2,1)}, u32[]{:S(2)}) copy-start(bf16[256,1024]{1,0:T(8,128)(2,1)} %v_ref.1) | copy-start | bytes 1572868
  34.4 2.1 %collective-permute-start.14 = (bf16[256,1024]{1,0:T(8,128)(2,1)}, bf16[256,1024]{1,0:T(8,128)(2,1)S(1)}, u32[]{:S(2)}, u32[]{:S(2)}) collective-permute-start(bf16[256,1024]{1,0:T(8,128)(2,1)} %collective-permute-done.3.refs_3_.refs_1_), channel_id=1, source_target_pairs={{0,1},{1,0},{2,3},{3,2},{4,5},{5,4},{6,7},{7,6},{8,9},{9,8},{10,11... | collective-permute-start | bytes 1572872 | tf_op jit(solution)/shard_map/ppermute | solution.py:244
  34.4 18.2 %collective-permute-start.9 = (bf16[256,1024]{1,0:T(8,128)(2,1)}, bf16[256,1024]{1,0:T(8,128)(2,1)S(1)}, u32[]{:S(2)}, u32[]{:S(2)}) collective-permute-start(bf16[256,1024]{1,0:T(8,128)(2,1)} %collective-permute-done.3.refs_3_.refs_1_), channel_id=1, source_target_pairs={{0,2},{1,3},{2,0},{3,1},{4,6},{5,7},{6,4},{7,5},{8,10},{9,11},{10,... | collective-permute-start | bytes 1572872 | tf_op jit(solution)/shard_map/ppermute | solution.py:244
  35.4 4.8 %collective-permute-start.15 = (bf16[256,1024]{1,0:T(8,128)(2,1)S(1)}, bf16[256,1024]{1,0:T(8,128)(2,1)S(1)}, u32[]{:S(2)}, u32[]{:S(2)}) collective-permute-start(bf16[256,1024]{1,0:T(8,128)(2,1)S(1)} %collective-permute-done.6.refs_4_), channel_id=1, source_target_pairs={{0,1},{1,0},{2,3},{3,2},{4,5},{5,4},{6,7},{7,6},{8,9},{9,8},{10,11... | collective-permute-start | bytes 1572872 | tf_op jit(solution)/shard_map/ppermute | solution.py:244
  35.6 14.2 %collective-permute-start.10 = (bf16[256,1024]{1,0:T(8,128)(2,1)S(1)}, bf16[256,1024]{1,0:T(8,128)(2,1)S(1)}, u32[]{:S(2)}, u32[]{:S(2)}) collective-permute-start(bf16[256,1024]{1,0:T(8,128)(2,1)S(1)} %broadcast_select_fusion.3), channel_id=1, source_target_pairs={{0,4},{1,5},{2,6},{3,7},{4,0},{5,1},{6,2},{7,3},{8,12},{9,13},{10,... | collective-permute-start | bytes 1572872 | tf_op jit(solution)/shard_map/ppermute | solution.py:244
  36.2 4.1 %collective-permute-start.13 = (bf16[256,1024]{1,0:T(8,128)(2,1)S(1)}, bf16[256,1024]{1,0:T(8,128)(2,1)S(1)}, u32[]{:S(2)}, u32[]{:S(2)}) collective-permute-start(bf16[256,1024]{1,0:T(8,128)(2,1)S(1)} %collective-permute-done.12.refs_2_), channel_id=1, source_target_pairs={{0,1},{1,0},{2,3},{3,2},{4,5},{5,4},{6,7},{7,6},{8,9},{9,8},{10,11... | collective-permute-start | bytes 1572872 | tf_op jit(solution)/shard_map/ppermute | solution.py:244
  36.3 3.9 %copy-start.2 = (bf16[256,1024]{1,0:T(8,128)(2,1)S(1)}, bf16[256,1024]{1,0:T(8,128)(2,1)}, u32[]{:S(2)}) copy-start(bf16[256,1024]{1,0:T(8,128)(2,1)} %copy-done.1) | copy-start | bytes 1572868
  36.6 16.1 %collective-permute-start.11 = (bf16[256,1024]{1,0:T(8,128)(2,1)S(1)}, bf16[256,1024]{1,0:T(8,128)(2,1)S(1)}, u32[]{:S(2)}, u32[]{:S(2)}) collective-permute-start(bf16[256,1024]{1,0:T(8,128)(2,1)S(1)} %broadcast_select_fusion), channel_id=1, source_target_pairs={{0,8},{1,9},{2,10},{3,11},{4,12},{5,13},{6,14},{7,15},{8,16},{9,17... | collective-permute-start | bytes 1572872 | tf_op jit(solution)/shard_map/ppermute | solution.py:244
  40.2 18.9 %collective-permute-start.16 = (bf16[256,1024]{1,0:T(8,128)(2,1)S(1)}, bf16[256,1024]{1,0:T(8,128)(2,1)S(1)}, u32[]{:S(2)}, u32[]{:S(2)}) collective-permute-start(bf16[256,1024]{1,0:T(8,128)(2,1)S(1)} %copy-done.2), channel_id=1, source_target_pairs={{0,1},{1,0},{2,3},{3,2},{4,5},{5,4},{6,7},{7,6},{8,9},{9,8},{10,11... | collective-permute-start | bytes 1572872 | tf_op jit(solution)/shard_map/ppermute | solution.py:244
  52.7 6.5 %collective-permute-start.17 = (bf16[256,1024]{1,0:T(8,128)(2,1)S(1)}, bf16[256,1024]{1,0:T(8,128)(2,1)S(1)}, u32[]{:S(2)}, u32[]{:S(2)}) collective-permute-start(bf16[256,1024]{1,0:T(8,128)(2,1)S(1)} %collective-permute-done.9.refs_2_), channel_id=1, source_target_pairs={{0,1},{1,0},{2,3},{3,2},{4,5},{5,4},{6,7},{7,6},{8,9},{9,8},{10,11... | collective-permute-start | bytes 1572872 | tf_op jit(solution)/shard_map/ppermute | solution.py:244
  52.7 6.5 %collective-permute-start.18 = (bf16[256,1024]{1,0:T(8,128)(2,1)S(1)}, bf16[256,1024]{1,0:T(8,128)(2,1)S(1)}, u32[]{:S(2)}, u32[]{:S(2)}) collective-permute-start(bf16[256,1024]{1,0:T(8,128)(2,1)S(1)} %collective-permute-done.10.refs_3_), channel_id=1, source_target_pairs={{0,1},{1,0},{2,3},{3,2},{4,5},{5,4},{6,7},{7,6},{8,9},{9,8},{10,11... | collective-permute-start | bytes 1572872 | tf_op jit(solution)/shard_map/ppermute | solution.py:244
  53.2 6.0 %collective-permute-start.19 = (bf16[256,1024]{1,0:T(8,128)(2,1)S(1)}, bf16[256,1024]{1,0:T(8,128)(2,1)S(1)}, u32[]{:S(2)}, u32[]{:S(2)}) collective-permute-start(bf16[256,1024]{1,0:T(8,128)(2,1)S(1)} %collective-permute-done.11.refs_4_), channel_id=1, source_target_pairs={{0,1},{1,0},{2,3},{3,2},{4,5},{5,4},{6,7},{7,6},{8,9},{9,8},{10,11... | collective-permute-start | bytes 1572872 | tf_op jit(solution)/shard_map/ppermute | solution.py:244
where the time goes:
time: 66.5 us; the launch traced here: 65.4 us
  waiting for transfers between devices  27.3 us (41%)
  Pallas kernels  21.7 us (33%)
  starting transfers between devices  10.6 us (16%)
  other arithmetic  3.33 us (5%)
  local copies, waits for them, and re-layouts  2.1 us (3%)
    ppermute x20, waiting for transfers between devices, send(): return lax.ppermute(array, AXES, along[way])  27.3 us
    pallas_call x6, Pallas kernels, call(): pl.pallas_call(functools.partial(kernel, group), in_specs=[pl.BlockSpec(m...  21.7 us
    ppermute x20, starting transfers between devices, send(): return lax.ppermute(array, AXES, along[way])  10.6 us
    select_n x1, other arithmetic, shards(): across2, side2 = (w(odd_x == 0, keys, z1), w(odd_y == 0, keys, z1))  2.27 us
    unnamed x14, local copies, waits for them, and re-layouts  2.1 us
  transfers between devices with their start and end apart: 20, of which 6 were waited for; matrix products, arithmetic and copies ran while one was open for 4% of the time, Pallas kernels for 24%

commit v1 on v0

--- a/solution.py
+++ b/solution.py
@@ -14,7 +14,7 @@
 NEG = -1e30
 SCALE = HEAD_DIM ** -0.5 * math.log2(math.e)
 HEADS_STEP = 4
-VMEM_BYTES = 16 * 2**20
+VMEM_BYTES = 8 * 2**20
 HIGH = 2.0 ** 60
 barrier = lax.optimization_barrier
 
@@ -107,8 +107,11 @@
             k = jnp.concatenate(ks, axis=0)
             ok = [jnp.where(at + place >= start, 1.0, 0.0).astype(jnp.bfloat16) for place in places]
             v = jnp.concatenate([with_ones(v, o) for v, o in zip(vs, ok)], axis=0)
-            for i in range(h * group, (h + 1) * group):
-                s = scores(qs[i], k)
+            members = range(h * group, (h + 1) * group)
+            s_all = scores(jnp.concatenate([qs[i] for i in members], axis=0), k)
+            sums, w_all = [], []
+            for n, i in enumerate(members):
+                s = s_all[n * rows:(n + 1) * rows]
                 top, total, before = top_in[j * count + i], total_in[j * count + i], befores[i]
                 if exact:
                     key = lax.broadcasted_iota(jnp.int32, (rows, rows), 1)
@@ -118,13 +121,18 @@
                     back = jnp.exp2((top - new) * SCALE)
                     top, total, before = new, total * back, before * back
                 w = []
-                for n in range(k.shape[0] // HEAD_DIM):
-                    part = jnp.exp2((s[:, n * HEAD_DIM:(n + 1) * HEAD_DIM] - top) * SCALE).astype(jnp.bfloat16)
+                for m in range(k.shape[0] // HEAD_DIM):
+                    part = jnp.exp2((s[:, m * HEAD_DIM:(m + 1) * HEAD_DIM] - top) * SCALE).astype(jnp.bfloat16)
                     w.append(part)
                     if not exact:
                         high = part if high is None else jnp.maximum(high, part)
-                both = jnp.dot(jnp.concatenate(w, axis=1), v, preferred_element_type=jnp.float32)
-                put(j, i, total + both[:, HEAD_DIM:], both[:, :HEAD_DIM] + before, top if exact else None)
+                w_all.append(jnp.concatenate(w, axis=1))
+                sums.append((top if exact else None, total, before))
+            both_all = jnp.dot(jnp.concatenate(w_all, axis=0), v, preferred_element_type=jnp.float32)
+            for n, i in enumerate(members):
+                both = both_all[n * rows:(n + 1) * rows]
+                top, total, before = sums[n]
+                put(j, i, total + both[:, HEAD_DIM:], both[:, :HEAD_DIM] + before, top)
         return high
 
     def step(j, _):
@@ -169,15 +177,18 @@
 
 
 def choose_middle(plane, core, tiles):
-    x1, y1, x2, y2, z2 = tiles
-    pk, pv = pick(plane, x2, x2, y2, x2), pick(plane, z2, x1, y1, x1)
-    qk, qv = pick(plane, y2, y2, x2, y2), pick(plane, z2, z2, z2, y1)
-    return (pk, qk), (pv, qv)
-
-
-def devices_middle(mates, plane, core, base):
-    part = 1 - core if mates else core
-    return base - 2 * pick(plane, 3, 1, 2, 1) + part, pick(plane, -8, base - 4, base - 6, base - 4) + part
+    def half(x1, y1, x2, y2, z2):
+        pk, pv = pick(plane, x2, x2, y2, x2), pick(plane, z2, x1, y1, x1)
+        qk, qv = pick(plane, y2, y2, x2, y2), pick(plane, z2, z2, z2, y1)
+        return (pk, qk), (pv, qv)
+    a, b = half(*tiles[:5]), half(*tiles[5:])
+    return a[0] + b[0], a[1] + b[1]
+
+
+def devices_middle(plane, core, base):
+    p = base - 2 * pick(plane, 3, 1, 2, 1)
+    q = pick(plane, -8, base - 4, base - 6, base - 4)
+    return p + core, q + core, p + 1 - core, q + 1 - core
 
 
 def choose_last(plane, core, tiles):
@@ -213,17 +224,46 @@
         scratch_shapes=scratch,
         input_output_aliases={4: 1} if carry and not last else {},
         cost_estimate=pl.CostEstimate(
-            flops=8 * rows * keys * width, bytes_accessed=4 * rows * width, transcendentals=0
+            flops=8 * rows * keys * width, bytes_accessed=4 * keys * width, transcendentals=0
         ),
         compiler_params=pltpu.CompilerParams(vmem_limit_bytes=VMEM_BYTES),
     )(ids, *arrays)
+
+
+def mix_kernel(rule, ids, *refs):
+    rule(ids[0] % 4, *refs)
+
+
+def mix(rule, ids, arrays, count, flops=0):
+    vmem = pl.BlockSpec(memory_space=pltpu.VMEM)
+    return pl.pallas_call(
+        functools.partial(mix_kernel, rule),
+        in_specs=[pl.BlockSpec(memory_space=pltpu.SMEM)] + [vmem] * len(arrays),
+        out_specs=[vmem] * count,
+        out_shape=[jax.ShapeDtypeStruct(arrays[0].shape, arrays[0].dtype)] * count,
+        cost_estimate=pl.CostEstimate(flops=flops, bytes_accessed=arrays[0].size, transcendentals=0),
+        compiler_params=pltpu.CompilerParams(vmem_limit_bytes=VMEM_BYTES),
+    )(ids, *arrays)
+
+
+def mix_round2(plane, keys, z1, across, side):
+    across[...] = jnp.where(plane % 2 == 0, keys[...], z1[...])
+    side[...] = jnp.where(plane // 2 == 0, keys[...], z1[...])
+
+
+def mix_up(plane, x1, y1, up):
+    up[...] = jnp.where(plane == 1, y1[...], x1[...])
+
+
+def mix_round3(plane, x1, z2, y1, values, side, up):
+    side[...] = jnp.where(plane // 2 == 0, x1[...], z2[...])
+    up[...] = jnp.where(plane == 0, y1[...], values[...])
 
 
 def shards(queries, keys, values, doc_ids):
     rows = queries.shape[0]
     chips, cores = lax.axis_size("section"), lax.axis_size("attn")
     chip, core = lax.axis_index("section"), lax.axis_index("attn")
-    plane, odd_x, odd_y = chip % 4, chip % 2, (chip // 2) % 2
 
     def routes(target):
         return [
@@ -248,7 +288,6 @@
 
     ids = jnp.stack([chip, core, jnp.int32(cores)])
     docs = doc_ids.reshape(-1, HEAD_DIM)
-    w = jnp.where
 
     def far(choose, devices, carry, pieces, keys, last=False):
         kernel = functools.partial(far_kernel, choose, devices, last)
@@ -257,22 +296,23 @@
     z1 = send(keys, "first_z")
     x1, y1 = send(values, "x"), send(values, "y")
     mate_k, mate_v = send(keys, "first_mate"), send(values, "first_mate")
-    z1, mate_k, mate_v = barrier((z1, mate_k, mate_v))
-    across2, side2 = w(odd_x == 0, keys, z1), w(odd_y == 0, keys, z1)
+    carry = call(own_kernel, ids, docs, queries, (), [keys, values], rows)
+    z1, mate_k, mate_v, *carry = barrier((z1, mate_k, mate_v, *carry))
+    across2, side2 = mix(mix_round2, ids, [keys, z1], 2)
     x2, y2 = send(across2, "x"), send(side2, "y")
     x1, y1, _, _ = barrier((x1, y1, across2, side2))
-    z2 = send(w(plane == 1, y1, x1), "z")
+    (up2,) = mix(mix_up, ids, [x1, y1], 1, 2 * 10**10)
+    z2 = send(up2, "z")
     x1s, y1s = swap(x1, y1)
-    carry = call(own_kernel, ids, docs, queries, (), [keys, values], rows)
-    carry = far(choose_first, devices_first, carry, [mate_k, mate_v], rows)
+    carry = far(choose_first, devices_first, carry, [mate_k, mate_v], 0)
     y2, z2, y1, x1s, y1s, *carry = barrier((y2, z2, y1, x1s, y1s, *carry))
     x3 = send(y2, "x")
-    side3, up3 = w(odd_y == 0, x1, z2), w(plane == 0, y1, values)
+    side3, up3 = mix(mix_round3, ids, [x1, z2, y1, values], 2, 2 * 10**10)
     y3, z3 = send(side3, "y"), send(up3, "z")
     x2s, y2s, z2s = swap(x2, y2, z2)
-    carry = far(choose_middle, functools.partial(devices_middle, False), carry, [x1, y1, x2, y2, z2], 2 * rows)
-    x2s, y2s, z2s, *carry = barrier((x2s, y2s, z2s, *carry))
-    carry = far(choose_middle, functools.partial(devices_middle, True), carry, [x1s, y1s, x2s, y2s, z2s], 2 * rows)
+    carry = far(
+        choose_middle, devices_middle, carry, [x1, y1, x2, y2, z2, x1s, y1s, x2s, y2s, z2s], 0
+    )
     x3, y3, z3, *carry = barrier((x3, y3, z3, *carry))
     z1s, x3s, y3s, z3s = swap(z1, x3, y3, z3)
     carry = far(choose_last, functools.partial(devices_last, False), carry, [z1, y2, x3, y3, z3], 2 * rows)

time: 66.5 us -> 64.5 us (0.970)
  waiting for transfers between devices: 27.3 us -> 21.7 us
  Pallas kernels: 21.7 us -> 25.8 us
  other arithmetic: 3.33 us -> 0.08 us
  local copies, waits for them, and re-layouts: 2.1 us -> 4.27 us
  starting transfers between devices: 10.6 us -> 11.8 us
    ppermute x20, waiting for transfers between devices: 27.3 us -> 21.7 us  [send(): return lax.ppermute(array, AXES, along[way])]
    select_n x4 -> x0, other arithmetic: 3.25 us -> none  [the longest x1 2.27 us: shards(): across2, side2 = (w(odd_x == 0, keys, z1), w(odd_y == 0, keys, z1))]
    unnamed x14 -> x16, local copies, waits for them, and re-layouts: 2.1 us -> 4.27 us
    pallas_call x6 -> x5, Pallas kernels: 21.7 us -> 23.8 us  [call(): pl.pallas_call(functools.partial(kernel, group), in_specs=[pl.BlockSpec(m...]
    pallas_call x0 -> x3, Pallas kernels: none -> 1.94 us  [mix(): pl.pallas_call(functools.partial(mix_kernel, rule), in_specs=[pl.BlockSpe...]
    ppermute x20, starting transfers between devices: 10.6 us -> 11.8 us  [send(): return lax.ppermute(array, AXES, along[way])]
  transfers between devices with their start and end apart: 20 -> 20, of which waited for: 6 -> 6; matrix products, arithmetic and copies ran while one was open for 4% -> 0% of each run, Pallas kernels for 24% -> 30%
where the time goes in v1:
time: 64.5 us; the launch traced here: 63.9 us
  Pallas kernels  25.8 us (40%)
  waiting for transfers between devices  21.7 us (34%)
  starting transfers between devices  11.8 us (18%)
  local copies, waits for them, and re-layouts  4.27 us (7%)
    pallas_call x5, Pallas kernels, call(): pl.pallas_call(functools.partial(kernel, group), in_specs=[pl.BlockSpec(m...  23.8 us
    ppermute x20, waiting for transfers between devices, send(): return lax.ppermute(array, AXES, along[way])  21.7 us
    ppermute x20, starting transfers between devices, send(): return lax.ppermute(array, AXES, along[way])  11.8 us
    unnamed x16, local copies, waits for them, and re-layouts  4.27 us
    pallas_call x3, Pallas kernels, mix(): pl.pallas_call(functools.partial(mix_kernel, rule), in_specs=[pl.BlockSpe...  1.94 us
  transfers between devices with their start and end apart: 20, of which 6 were waited for; matrix products, arithmetic and copies ran while one was open for 0% of the time, Pallas kernels for 30%

profile of v1, /device:TPU:4, one launch (start us, length us, event | category | flops | bytes accessed | tf_op | source)
XLA Modules:
  0.0 63.9 jit_solution(7800208413260608265)
XLA Ops:
  0.0 1.6 %collective-permute-start = (bf16[256,1024]{1,0:T(8,128)(2,1)}, bf16[256,1024]{1,0:T(8,128)(2,1)S(1)}, u32[]{:S(2)}, u32[]{:S(2)}) collective-permute-start(bf16[256,1024]{1,0:T(8,128)(2,1)} %refs_0_.1), channel_id=1, source_target_pairs={{0,1},{1,0},{2,10},{3,11},{4,12},{5,13},{6,14},{7,15},{8,9},{9,8},... | collective-permute-start | bytes 1572872 | tf_op jit(solution)/shard_map/ppermute | solution.py:284
  1.6 0.0 collective-permute-start.1
  1.6 0.5 collective-permute-start.2
  2.1 1.5 %collective-permute-start.4 = (bf16[256,1024]{1,0:T(8,128)(2,1)}, bf16[256,1024]{1,0:T(8,128)(2,1)S(1)}, u32[]{:S(2)}, u32[]{:S(2)}) collective-permute-start(bf16[256,1024]{1,0:T(8,128)(2,1)} %refs_3_.1), channel_id=1, source_target_pairs={{0,2},{1,3},{2,0},{3,1},{4,6},{5,7},{6,4},{7,5},{8,10},{9,11},{10,... | collective-permute-start | bytes 1572872 | tf_op jit(solution)/shard_map/ppermute | solution.py:284
  3.6 0.5 collective-permute-start.5
  4.1 0.1 pad_add_fusion.ids
  4.2 0.0 copy-start
  4.2 1.4 %copy-done = bf16[256,3072]{1,0:T(8,128)(2,1)S(1)} copy-done((bf16[256,3072]{1,0:T(8,128)(2,1)S(1)}, bf16[256,3072]{1,0:T(8,128)(2,1)}, u32[]{:S(2)}) %copy-start) | copy-done | bytes 1572888
  5.6 0.0 copy-start.2
  5.6 0.8 %copy-done.2 = s32[8192]{0:T(1024)S(1)} copy-done((s32[8192]{0:T(1024)S(1)}, s32[8192]{0:T(1024)}, u32[]{:S(2)}) %copy-start.2) | copy-done | bytes 32792
  6.3 0.0 copy-start.4
  6.3 1.0 %copy-done.4 = bf16[256,1024]{1,0:T(8,128)(2,1)S(1)} copy-done((bf16[256,1024]{1,0:T(8,128)(2,1)S(1)}, bf16[256,1024]{1,0:T(8,128)(2,1)}, u32[]{:S(2)}) %copy-start.4) | copy-done | bytes 524312
  7.4 0.0 copy-start.6
  7.4 1.0 %copy-done.6 = bf16[256,1024]{1,0:T(8,128)(2,1)S(1)} copy-done((bf16[256,1024]{1,0:T(8,128)(2,1)S(1)}, bf16[256,1024]{1,0:T(8,128)(2,1)}, u32[]{:S(2)}) %copy-start.6) | copy-done | bytes 524312
  8.4 0.0 copy-start.5
  8.4 3.1 %shard_map.46 = (f32[256,3072]{1,0:T(8,128)S(1)}, f32[24,256,128]{2,1,0:T(8,128)S(1)}, f32[24,256,128]{2,1,0:T(8,128)S(1)}) custom-call(s32[3]{0:T(128)S(1)} %pad_add_fusion.ids, s32[64,128]{1,0:T(8,128)S(1)} %bitcast.3, bf16[256,3072]{1,0:T(8,128)(2,1)S(1)} %copy-done, bf16[256,1024]{1,0:T(8,128)(2,1)S(1)} %copy-done.4, bf16[256,1024]{1,0:T(8,128)(2,1)S(1)} %copy-done.6), custom_call_target="tpu_custom_call" | custom-call | flops 1610612736 | bytes 3145728 | tf_op jit(solution)/shard_map/pallas_call | solution.py:219
  11.5 4.2 %collective-permute-done.refs_1_.refs_0_ = bf16[256,1024]{1,0:T(8,128)(2,1)S(1)} collective-permute-done((bf16[256,1024]{1,0:T(8,128)(2,1)}, bf16[256,1024]{1,0:T(8,128)(2,1)S(1)}, u32[]{:S(2)}, u32[]{:S(2)}) %collective-permute-start) | collective-permute-done | bytes 524320 | tf_op jit(solution)/shard_map/ppermute | solution.py:284
  15.7 0.0 collective-permute-done.1.refs_0_
  15.7 0.0 collective-permute-done.2.refs_1_
  15.7 0.0 copy-done.5
  15.7 0.7 %shard_map.47 = (bf16[256,1024]{1,0:T(8,128)(2,1)S(1)}, bf16[256,1024]{1,0:T(8,128)(2,1)S(1)}) custom-call(s32[3]{0:T(128)S(1)} %pad_add_fusion.ids, bf16[256,1024]{1,0:T(8,128)(2,1)S(1)} %copy-done.5, bf16[256,1024]{1,0:T(8,128)(2,1)S(1)} %collective-permute-done.refs_1_.refs_0_), custom_call_target="tpu_custom_call" | custom-call | bytes 262144 | tf_op jit(solution)/shard_map/pallas_call | solution.py:239
  16.4 0.0 collective-permute-done.4.refs_0_
  16.4 0.9 %collective-permute-done.5.refs_1_.refs_2_ = bf16[256,1024]{1,0:T(8,128)(2,1)S(1)} collective-permute-done((bf16[256,1024]{1,0:T(8,128)(2,1)}, bf16[256,1024]{1,0:T(8,128)(2,1)S(1)}, u32[]{:S(2)}, u32[]{:S(2)}) %collective-permute-start.5) | collective-permute-done | bytes 524320 | tf_op jit(solution)/shard_map/ppermute | solution.py:284
  17.3 0.0 copy-start.1
  17.3 0.6 shard_map.48
  18.0 0.0 copy-start.7
  18.0 1.6 %collective-permute-start.6 = (bf16[256,1024]{1,0:T(8,128)(2,1)S(1)}, bf16[256,1024]{1,0:T(8,128)(2,1)S(1)}, u32[]{:S(2)}, u32[]{:S(2)}) collective-permute-start(bf16[256,1024]{1,0:T(8,128)(2,1)S(1)} %shard_map.48), channel_id=1, source_target_pairs={{0,8},{1,9},{2,10},{3,11},{4,12},{5,13},{6,14},{7,15},{8,16},{9,17... | collective-permute-start | bytes 1572872 | tf_op jit(solution)/shard_map/ppermute | solution.py:284
  19.6 0.0 collective-permute-start.7
  19.6 0.5 collective-permute-start.8
  20.1 0.5 collective-permute-start.3
  20.6 0.6 %collective-permute-start.12 = (bf16[256,1024]{1,0:T(8,128)(2,1)S(1)}, bf16[256,1024]{1,0:T(8,128)(2,1)S(1)}, u32[]{:S(2)}, u32[]{:S(2)}) collective-permute-start(bf16[256,1024]{1,0:T(8,128)(2,1)S(1)} %get-tuple-element.48), channel_id=1, source_target_pairs={{0,2},{1,3},{2,0},{3,1},{4,6},{5,7},{6,4},{7,5},{8,10},{9,11},{10,... | collective-permute-start | bytes 1572872 | tf_op jit(solution)/shard_map/ppermute | solution.py:284
  21.3 0.0 copy-done.1
  21.3 0.0 copy-done.3
  21.3 1.6 %shard_map.49 = (f32[256,3072]{1,0:T(8,128)S(1)}, f32[24,256,128]{2,1,0:T(8,128)S(1)}, f32[24,256,128]{2,1,0:T(8,128)S(1)}) custom-call(s32[3]{0:T(128)S(1)} %pad_add_fusion.ids, s32[64,128]{1,0:T(8,128)S(1)} %bitcast.4, bf16[256,3072]{1,0:T(8,128)(2,1)S(1)} %copy-done.1, f32[256,3072]{1,0:T(8,128)S(1)} %get-tuple-element.51.acc_in, ...), custom_call_target="tpu_custom_call", output_to_operand_aliasing={{1}: (4, {})} | custom-call | tf_op jit(solution)/shard_map/pallas_call | solution.py:219
  22.9 9.6 %collective-permute-done.6.refs_1_.refs_4_ = bf16[256,1024]{1,0:T(8,128)(2,1)S(1)} collective-permute-done((bf16[256,1024]{1,0:T(8,128)(2,1)S(1)}, bf16[256,1024]{1,0:T(8,128)(2,1)S(1)}, u32[]{:S(2)}, u32[]{:S(2)}) %collective-permute-start.6) | collective-permute-done | bytes 524320 | tf_op jit(solution)/shard_map/ppermute | solution.py:284
  32.5 0.0 collective-permute-done.7.refs_5_
  32.5 0.0 collective-permute-done.8.refs_6_
  32.5 1.5 %collective-permute-done.3.refs_3_.refs_1_ = bf16[256,1024]{1,0:T(8,128)(2,1)S(1)} collective-permute-done((bf16[256,1024]{1,0:T(8,128)(2,1)S(1)}, bf16[256,1024]{1,0:T(8,128)(2,1)S(1)}, u32[]{:S(2)}, u32[]{:S(2)}) %collective-permute-start.3) | collective-permute-done | bytes 524320 | tf_op jit(solution)/shard_map/ppermute | solution.py:284
  33.9 0.0 collective-permute-start.14
  33.9 0.5 collective-permute-start.15
  34.4 0.0 collective-permute-done.12.refs_2_
  34.5 0.0 collective-permute-start.13
  34.5 0.0 copy-done.7
  34.5 0.7 %shard_map.50 = (bf16[256,1024]{1,0:T(8,128)(2,1)S(1)}, bf16[256,1024]{1,0:T(8,128)(2,1)S(1)}) custom-call(s32[3]{0:T(128)S(1)} %pad_add_fusion.ids, bf16[256,1024]{1,0:T(8,128)(2,1)S(1)} %collective-permute-done.4.refs_0_, bf16[256,1024]{1,0:T(8,128)(2,1)S(1)} %collective-permute-done.6.refs_1_.refs_4_, ...), custom_call_target="tpu_custom_call" | custom-call | flops 20000000000 | bytes 262144 | tf_op jit(solution)/shard_map/pallas_call | solution.py:239
  35.2 1.3 %collective-permute-start.10 = (bf16[256,1024]{1,0:T(8,128)(2,1)S(1)}, bf16[256,1024]{1,0:T(8,128)(2,1)S(1)}, u32[]{:S(2)}, u32[]{:S(2)}) collective-permute-start(bf16[256,1024]{1,0:T(8,128)(2,1)S(1)} %get-tuple-element.62), channel_id=1, source_target_pairs={{0,4},{1,5},{2,6},{3,7},{4,0},{5,1},{6,2},{7,3},{8,12},{9,13},{10,... | collective-permute-start | bytes 1572872 | tf_op jit(solution)/shard_map/ppermute | solution.py:284
  36.4 1.6 %collective-permute-start.11 = (bf16[256,1024]{1,0:T(8,128)(2,1)S(1)}, bf16[256,1024]{1,0:T(8,128)(2,1)S(1)}, u32[]{:S(2)}, u32[]{:S(2)}) collective-permute-start(bf16[256,1024]{1,0:T(8,128)(2,1)S(1)} %get-tuple-element.63), channel_id=1, source_target_pairs={{0,8},{1,9},{2,10},{3,11},{4,12},{5,13},{6,14},{7,15},{8,16},{9,17... | collective-permute-start | bytes 1572872 | tf_op jit(solution)/shard_map/ppermute | solution.py:284
  38.0 0.0 collective-permute-done.14.refs_8_.refs_1_
  38.0 0.5 collective-permute-start.9
  38.6 0.0 collective-permute-done.15.refs_9_
  38.6 0.0 collective-permute-start.16
  38.6 0.0 collective-permute-done.13.refs_7_
  38.6 8.3 %shard_map.51 = (f32[256,3072]{1,0:T(8,128)S(1)}, f32[24,256,128]{2,1,0:T(8,128)S(1)}, f32[24,256,128]{2,1,0:T(8,128)S(1)}) custom-call(s32[3]{0:T(128)S(1)} %pad_add_fusion.ids, s32[64,128]{1,0:T(8,128)S(1)} %bitcast.5, bf16[256,3072]{1,0:T(8,128)(2,1)S(1)} %copy-done.1, f32[256,3072]{1,0:T(8,128)S(1)} %get-tuple-element.64.acc_in, ...), custom_call_target="tpu_custom_call", output_to_operand_aliasing={{1}: (4, {})} | custom-call | tf_op jit(solution)/shard_map/pallas_call | solution.py:219
  46.9 2.7 %collective-permute-done.10.refs_3_ = bf16[256,1024]{1,0:T(8,128)(2,1)S(1)} collective-permute-done((bf16[256,1024]{1,0:T(8,128)(2,1)S(1)}, bf16[256,1024]{1,0:T(8,128)(2,1)S(1)}, u32[]{:S(2)}, u32[]{:S(2)}) %collective-permute-start.10) | collective-permute-done | bytes 524320 | tf_op jit(solution)/shard_map/ppermute | solution.py:284
  49.5 2.8 %collective-permute-done.11.refs_4_ = bf16[256,1024]{1,0:T(8,128)(2,1)S(1)} collective-permute-done((bf16[256,1024]{1,0:T(8,128)(2,1)S(1)}, bf16[256,1024]{1,0:T(8,128)(2,1)S(1)}, u32[]{:S(2)}, u32[]{:S(2)}) %collective-permute-start.11) | collective-permute-done | bytes 524320 | tf_op jit(solution)/shard_map/ppermute | solution.py:284
  52.3 0.0 collective-permute-done.9.refs_2_
  52.3 0.0 collective-permute-start.17
  52.3 0.5 collective-permute-start.18
  52.8 0.0 collective-permute-start.19
  52.8 5.1 %shard_map.52 = (f32[256,3072]{1,0:T(8,128)S(1)}, f32[24,256,128]{2,1,0:T(8,128)S(1)}, f32[24,256,128]{2,1,0:T(8,128)S(1)}) custom-call(s32[3]{0:T(128)S(1)} %pad_add_fusion.ids, s32[64,128]{1,0:T(8,128)S(1)} %bitcast.6, bf16[256,3072]{1,0:T(8,128)(2,1)S(1)} %copy-done.1, f32[256,3072]{1,0:T(8,128)S(1)} %get-tuple-element.72.acc_in, ...), custom_call_target="tpu_custom_call", output_to_operand_aliasing={{1}: (4, {})} | custom-call | flops 3221225472 | bytes 6291456 | tf_op jit(solution)/shard_map/pallas_call | solution.py:219
  57.9 0.0 collective-permute-done.16.refs_0_
  57.9 0.0 collective-permute-done.17.refs_2_
  57.9 0.0 collective-permute-done.18.refs_3_
  57.9 0.0 collective-permute-done.19.refs_4_
  57.9 5.8 %shard_map.53 = bf16[256,3072]{1,0:T(8,128)(2,1)} custom-call(s32[3]{0:T(128)S(1)} %pad_add_fusion.ids, s32[64,128]{1,0:T(8,128)S(1)} %bitcast.7, bf16[256,3072]{1,0:T(8,128)(2,1)S(1)} %copy-done.1, f32[256,3072]{1,0:T(8,128)S(1)} %get-tuple-element.78.acc_in, f32[24,256,128]{2,1,0:T(8,128)S(1)} %get-tuple-element.79.top_in, ...), custom_call_target="tpu_custom_call" | custom-call | flops 3221225472 | bytes 6291456 | tf_op jit(solution)/shard_map/pallas_call | solution.py:219
  (1 shorter events, 0.0 us)
Async XLA Ops:
  0.0 15.7 %collective-permute-start = (bf16[256,1024]{1,0:T(8,128)(2,1)}, bf16[256,1024]{1,0:T(8,128)(2,1)S(1)}, u32[]{:S(2)}, u32[]{:S(2)}) collective-permute-start(bf16[256,1024]{1,0:T(8,128)(2,1)} %refs_0_.1), channel_id=1, source_target_pairs={{0,1},{1,0},{2,10},{3,11},{4,12},{5,13},{6,14},{7,15},{8,9},{9,8},... | collective-permute-start | bytes 1572872 | tf_op jit(solution)/shard_map/ppermute | solution.py:284
  1.6 14.2 %collective-permute-start.1 = (bf16[256,1024]{1,0:T(8,128)(2,1)}, bf16[256,1024]{1,0:T(8,128)(2,1)S(1)}, u32[]{:S(2)}, u32[]{:S(2)}) collective-permute-start(bf16[256,1024]{1,0:T(8,128)(2,1)} %refs_0_.1), channel_id=1, source_target_pairs={{0,1},{1,8},{2,3},{3,2},{4,5},{5,4},{6,7},{7,6},{8,9},{9,16},{10,1... | collective-permute-start | bytes 1572872 | tf_op jit(solution)/shard_map/ppermute | solution.py:284
  1.6 14.2 %collective-permute-start.2 = (bf16[256,1024]{1,0:T(8,128)(2,1)}, bf16[256,1024]{1,0:T(8,128)(2,1)S(1)}, u32[]{:S(2)}, u32[]{:S(2)}) collective-permute-start(bf16[256,1024]{1,0:T(8,128)(2,1)} %refs_3_.1), channel_id=1, source_target_pairs={{0,1},{1,8},{2,3},{3,2},{4,5},{5,4},{6,7},{7,6},{8,9},{9,16},{10,1... | collective-permute-start | bytes 1572872 | tf_op jit(solution)/shard_map/ppermute | solution.py:284
  2.1 14.3 %collective-permute-start.4 = (bf16[256,1024]{1,0:T(8,128)(2,1)}, bf16[256,1024]{1,0:T(8,128)(2,1)S(1)}, u32[]{:S(2)}, u32[]{:S(2)}) collective-permute-start(bf16[256,1024]{1,0:T(8,128)(2,1)} %refs_3_.1), channel_id=1, source_target_pairs={{0,2},{1,3},{2,0},{3,1},{4,6},{5,7},{6,4},{7,5},{8,10},{9,11},{10,... | collective-permute-start | bytes 1572872 | tf_op jit(solution)/shard_map/ppermute | solution.py:284
  3.6 13.8 %collective-permute-start.5 = (bf16[256,1024]{1,0:T(8,128)(2,1)}, bf16[256,1024]{1,0:T(8,128)(2,1)S(1)}, u32[]{:S(2)}, u32[]{:S(2)}) collective-permute-start(bf16[256,1024]{1,0:T(8,128)(2,1)} %refs_3_.1), channel_id=1, source_target_pairs={{0,4},{1,5},{2,6},{3,7},{4,0},{5,1},{6,2},{7,3},{8,12},{9,13},{10,... | collective-permute-start | bytes 1572872 | tf_op jit(solution)/shard_map/ppermute | solution.py:284
  4.2 1.4 %copy-start = (bf16[256,3072]{1,0:T(8,128)(2,1)S(1)}, bf16[256,3072]{1,0:T(8,128)(2,1)}, u32[]{:S(2)}) copy-start(bf16[256,3072]{1,0:T(8,128)(2,1)} %q_ref.9) | copy-start | bytes 4718596
  5.6 0.8 %copy-start.2 = (s32[8192]{0:T(1024)S(1)}, s32[8192]{0:T(1024)}, u32[]{:S(2)}) copy-start(s32[8192]{0:T(1024)} %param.7) | copy-start | bytes 98308
  6.3 1.0 %copy-start.4 = (bf16[256,1024]{1,0:T(8,128)(2,1)S(1)}, bf16[256,1024]{1,0:T(8,128)(2,1)}, u32[]{:S(2)}) copy-start(bf16[256,1024]{1,0:T(8,128)(2,1)} %refs_0_.1) | copy-start | bytes 1572868
  7.4 1.0 %copy-start.6 = (bf16[256,1024]{1,0:T(8,128)(2,1)S(1)}, bf16[256,1024]{1,0:T(8,128)(2,1)}, u32[]{:S(2)}) copy-start(bf16[256,1024]{1,0:T(8,128)(2,1)} %refs_3_.1) | copy-start | bytes 1572868
  8.4 7.3 %copy-start.5 = (bf16[256,1024]{1,0:T(8,128)(2,1)S(1)}, bf16[256,1024]{1,0:T(8,128)(2,1)}, u32[]{:S(2)}) copy-start(bf16[256,1024]{1,0:T(8,128)(2,1)} %refs_0_.1) | copy-start | bytes 1572868
  17.3 3.9 %copy-start.1 = (bf16[256,3072]{1,0:T(8,128)(2,1)S(1)}, bf16[256,3072]{1,0:T(8,128)(2,1)}, u32[]{:S(2)}) copy-start(bf16[256,3072]{1,0:T(8,128)(2,1)} %q_ref.9) | copy-start | bytes 4718596
  17.3 3.9 %copy-start.3 = (s32[8192]{0:T(1024)S(1)}, s32[8192]{0:T(1024)}, u32[]{:S(2)}) copy-start(s32[8192]{0:T(1024)} %param.7) | copy-start | bytes 98308
  18.0 16.5 %copy-start.7 = (bf16[256,1024]{1,0:T(8,128)(2,1)S(1)}, bf16[256,1024]{1,0:T(8,128)(2,1)}, u32[]{:S(2)}) copy-start(bf16[256,1024]{1,0:T(8,128)(2,1)} %refs_3_.1) | copy-start | bytes 1572868
  18.0 14.5 %collective-permute-start.6 = (bf16[256,1024]{1,0:T(8,128)(2,1)S(1)}, bf16[256,1024]{1,0:T(8,128)(2,1)S(1)}, u32[]{:S(2)}, u32[]{:S(2)}) collective-permute-start(bf16[256,1024]{1,0:T(8,128)(2,1)S(1)} %shard_map.48), channel_id=1, source_target_pairs={{0,8},{1,9},{2,10},{3,11},{4,12},{5,13},{6,14},{7,15},{8,16},{9,17... | collective-permute-start | bytes 1572872 | tf_op jit(solution)/shard_map/ppermute | solution.py:284
  19.6 12.9 %collective-permute-start.7 = (bf16[256,1024]{1,0:T(8,128)(2,1)S(1)}, bf16[256,1024]{1,0:T(8,128)(2,1)S(1)}, u32[]{:S(2)}, u32[]{:S(2)}) collective-permute-start(bf16[256,1024]{1,0:T(8,128)(2,1)S(1)} %collective-permute-done.4.refs_0_), channel_id=1, source_target_pairs={{0,1},{1,0},{2,3},{3,2},{4,5},{5,4},{6,7},{7,6},{8,9},{9,8},{10,11... | collective-permute-start | bytes 1572872 | tf_op jit(solution)/shard_map/ppermute | solution.py:284
  19.6 12.9 %collective-permute-start.8 = (bf16[256,1024]{1,0:T(8,128)(2,1)S(1)}, bf16[256,1024]{1,0:T(8,128)(2,1)S(1)}, u32[]{:S(2)}, u32[]{:S(2)}) collective-permute-start(bf16[256,1024]{1,0:T(8,128)(2,1)S(1)} %collective-permute-done.5.refs_1_.refs_2_), channel_id=1, source_target_pairs={{0,1},{1,0},{2,3},{3,2},{4,5},{5,4},{6,7},{7,6},{8,9},{9,8},{10,11... | collective-permute-start | bytes 1572872 | tf_op jit(solution)/shard_map/ppermute | solution.py:284
  20.1 13.8 %collective-permute-start.3 = (bf16[256,1024]{1,0:T(8,128)(2,1)S(1)}, bf16[256,1024]{1,0:T(8,128)(2,1)S(1)}, u32[]{:S(2)}, u32[]{:S(2)}) collective-permute-start(bf16[256,1024]{1,0:T(8,128)(2,1)S(1)} %get-tuple-element.47), channel_id=1, source_target_pairs={{0,4},{1,5},{2,6},{3,7},{4,0},{5,1},{6,2},{7,3},{8,12},{9,13},{10,... | collective-permute-start | bytes 1572872 | tf_op jit(solution)/shard_map/ppermute | solution.py:284
  20.6 13.8 %collective-permute-start.12 = (bf16[256,1024]{1,0:T(8,128)(2,1)S(1)}, bf16[256,1024]{1,0:T(8,128)(2,1)S(1)}, u32[]{:S(2)}, u32[]{:S(2)}) collective-permute-start(bf16[256,1024]{1,0:T(8,128)(2,1)S(1)} %get-tuple-element.48), channel_id=1, source_target_pairs={{0,2},{1,3},{2,0},{3,1},{4,6},{5,7},{6,4},{7,5},{8,10},{9,11},{10,... | collective-permute-start | bytes 1572872 | tf_op jit(solution)/shard_map/ppermute | solution.py:284
  33.9 4.1 %collective-permute-start.14 = (bf16[256,1024]{1,0:T(8,128)(2,1)S(1)}, bf16[256,1024]{1,0:T(8,128)(2,1)S(1)}, u32[]{:S(2)}, u32[]{:S(2)}) collective-permute-start(bf16[256,1024]{1,0:T(8,128)(2,1)S(1)} %collective-permute-done.3.refs_3_.refs_1_), channel_id=1, source_target_pairs={{0,1},{1,0},{2,3},{3,2},{4,5},{5,4},{6,7},{7,6},{8,9},{9,8},{10,11... | collective-permute-start | bytes 1572872 | tf_op jit(solution)/shard_map/ppermute | solution.py:284
  33.9 4.6 %collective-permute-start.15 = (bf16[256,1024]{1,0:T(8,128)(2,1)S(1)}, bf16[256,1024]{1,0:T(8,128)(2,1)S(1)}, u32[]{:S(2)}, u32[]{:S(2)}) collective-permute-start(bf16[256,1024]{1,0:T(8,128)(2,1)S(1)} %collective-permute-done.6.refs_1_.refs_4_), channel_id=1, source_target_pairs={{0,1},{1,0},{2,3},{3,2},{4,5},{5,4},{6,7},{7,6},{8,9},{9,8},{10,11... | collective-permute-start | bytes 1572872 | tf_op jit(solution)/shard_map/ppermute | solution.py:284
  34.5 4.1 %collective-permute-start.13 = (bf16[256,1024]{1,0:T(8,128)(2,1)S(1)}, bf16[256,1024]{1,0:T(8,128)(2,1)S(1)}, u32[]{:S(2)}, u32[]{:S(2)}) collective-permute-start(bf16[256,1024]{1,0:T(8,128)(2,1)S(1)} %collective-permute-done.12.refs_2_), channel_id=1, source_target_pairs={{0,1},{1,0},{2,3},{3,2},{4,5},{5,4},{6,7},{7,6},{8,9},{9,8},{10,11... | collective-permute-start | bytes 1572872 | tf_op jit(solution)/shard_map/ppermute | solution.py:284
  35.2 14.4 %collective-permute-start.10 = (bf16[256,1024]{1,0:T(8,128)(2,1)S(1)}, bf16[256,1024]{1,0:T(8,128)(2,1)S(1)}, u32[]{:S(2)}, u32[]{:S(2)}) collective-permute-start(bf16[256,1024]{1,0:T(8,128)(2,1)S(1)} %get-tuple-element.62), channel_id=1, source_target_pairs={{0,4},{1,5},{2,6},{3,7},{4,0},{5,1},{6,2},{7,3},{8,12},{9,13},{10,... | collective-permute-start | bytes 1572872 | tf_op jit(solution)/shard_map/ppermute | solution.py:284
  36.4 15.9 %collective-permute-start.11 = (bf16[256,1024]{1,0:T(8,128)(2,1)S(1)}, bf16[256,1024]{1,0:T(8,128)(2,1)S(1)}, u32[]{:S(2)}, u32[]{:S(2)}) collective-permute-start(bf16[256,1024]{1,0:T(8,128)(2,1)S(1)} %get-tuple-element.63), channel_id=1, source_target_pairs={{0,8},{1,9},{2,10},{3,11},{4,12},{5,13},{6,14},{7,15},{8,16},{9,17... | collective-permute-start | bytes 1572872 | tf_op jit(solution)/shard_map/ppermute | solution.py:284
  38.0 14.3 %collective-permute-start.9 = (bf16[256,1024]{1,0:T(8,128)(2,1)S(1)}, bf16[256,1024]{1,0:T(8,128)(2,1)S(1)}, u32[]{:S(2)}, u32[]{:S(2)}) collective-permute-start(bf16[256,1024]{1,0:T(8,128)(2,1)S(1)} %collective-permute-done.3.refs_3_.refs_1_), channel_id=1, source_target_pairs={{0,2},{1,3},{2,0},{3,1},{4,6},{5,7},{6,4},{7,5},{8,10},{9,11},{10,... | collective-permute-start | bytes 1572872 | tf_op jit(solution)/shard_map/ppermute | solution.py:284
  38.6 19.3 %collective-permute-start.16 = (bf16[256,1024]{1,0:T(8,128)(2,1)S(1)}, bf16[256,1024]{1,0:T(8,128)(2,1)S(1)}, u32[]{:S(2)}, u32[]{:S(2)}) collective-permute-start(bf16[256,1024]{1,0:T(8,128)(2,1)S(1)} %collective-permute-done.refs_1_.refs_0_), channel_id=1, source_target_pairs={{0,1},{1,0},{2,3},{3,2},{4,5},{5,4},{6,7},{7,6},{8,9},{9,8},{10,11... | collective-permute-start | bytes 1572872 | tf_op jit(solution)/shard_map/ppermute | solution.py:284
  52.3 5.6 %collective-permute-start.17 = (bf16[256,1024]{1,0:T(8,128)(2,1)S(1)}, bf16[256,1024]{1,0:T(8,128)(2,1)S(1)}, u32[]{:S(2)}, u32[]{:S(2)}) collective-permute-start(bf16[256,1024]{1,0:T(8,128)(2,1)S(1)} %collective-permute-done.9.refs_2_), channel_id=1, source_target_pairs={{0,1},{1,0},{2,3},{3,2},{4,5},{5,4},{6,7},{7,6},{8,9},{9,8},{10,11... | collective-permute-start | bytes 1572872 | tf_op jit(solution)/shard_map/ppermute | solution.py:284
  52.3 5.6 %collective-permute-start.18 = (bf16[256,1024]{1,0:T(8,128)(2,1)S(1)}, bf16[256,1024]{1,0:T(8,128)(2,1)S(1)}, u32[]{:S(2)}, u32[]{:S(2)}) collective-permute-start(bf16[256,1024]{1,0:T(8,128)(2,1)S(1)} %collective-permute-done.10.refs_3_), channel_id=1, source_target_pairs={{0,1},{1,0},{2,3},{3,2},{4,5},{5,4},{6,7},{7,6},{8,9},{9,8},{10,11... | collective-permute-start | bytes 1572872 | tf_op jit(solution)/shard_map/ppermute | solution.py:284
  52.8 5.1 %collective-permute-start.19 = (bf16[256,1024]{1,0:T(8,128)(2,1)S(1)}, bf16[256,1024]{1,0:T(8,128)(2,1)S(1)}, u32[]{:S(2)}, u32[]{:S(2)}) collective-permute-start(bf16[256,1024]{1,0:T(8,128)(2,1)S(1)} %collective-permute-done.11.refs_4_), channel_id=1, source_target_pairs={{0,1},{1,0},{2,3},{3,2},{4,5},{5,4},{6,7},{7,6},{8,9},{9,8},{10,11... | collective-permute-start | bytes 1572872 | tf_op jit(solution)/shard_map/ppermute | solution.py:284

commit v2 on v1

--- a/solution.py
+++ b/solution.py
@@ -75,7 +75,7 @@
     lax.fori_loop(0, k_ref.shape[1] // HEAD_DIM // HEADS_STEP, step, 0)
 
 
-def far_kernel(choose, devices, last, group, ids, docs_ref, q_ref, acc_in, top_in, total_in, *refs):
+def far_kernel(choose, devices, last, heads_step, group, ids, docs_ref, q_ref, acc_in, top_in, total_in, *refs):
     rows = q_ref.shape[0]
     chip, core, first, start, _ = where_am_i(ids, docs_ref, rows)
     plane, owner = chip % 4, first // rows
@@ -84,8 +84,8 @@
         refs, (hbm, acc_out, sems) = refs[:-3], refs[-3:]
     else:
         refs, (acc_out, top_out, total_out) = refs[:-3], refs[-3:]
-    count = HEADS_STEP * group
-    steps = refs[0].shape[1] // HEAD_DIM // HEADS_STEP
+    count = heads_step * group
+    steps = refs[0].shape[1] // HEAD_DIM // heads_step
     needed = functools.reduce(jnp.maximum, places) + rows > start
 
     def put(j, i, total, out, top=None):
@@ -99,10 +99,10 @@
 
     def attend(j, exact):
         qs, befores = heads_of(q_ref, j, count), heads_of(acc_in, j, count)
-        tiles = [heads_of(r, j, HEADS_STEP) for r in refs]
+        tiles = [heads_of(r, j, heads_step) for r in refs]
         at = lax.broadcasted_iota(jnp.int32, (rows, HEAD_DIM), 0)
         high = None
-        for h in range(HEADS_STEP):
+        for h in range(heads_step):
             ks, vs = choose(plane, core, [t[h] for t in tiles])
             k = jnp.concatenate(ks, axis=0)
             ok = [jnp.where(at + place >= start, 1.0, 0.0).astype(jnp.bfloat16) for place in places]
@@ -289,23 +289,23 @@
     ids = jnp.stack([chip, core, jnp.int32(cores)])
     docs = doc_ids.reshape(-1, HEAD_DIM)
 
-    def far(choose, devices, carry, pieces, keys, last=False):
-        kernel = functools.partial(far_kernel, choose, devices, last)
+    def far(choose, devices, carry, pieces, keys, last=False, heads_step=HEADS_STEP):
+        kernel = functools.partial(far_kernel, choose, devices, last, heads_step)
         return call(kernel, ids, docs, queries, carry, pieces, keys, last)
 
     z1 = send(keys, "first_z")
     x1, y1 = send(values, "x"), send(values, "y")
     mate_k, mate_v = send(keys, "first_mate"), send(values, "first_mate")
     carry = call(own_kernel, ids, docs, queries, (), [keys, values], rows)
-    z1, mate_k, mate_v, *carry = barrier((z1, mate_k, mate_v, *carry))
+    z1, *carry = barrier((z1, *carry))
     across2, side2 = mix(mix_round2, ids, [keys, z1], 2)
     x2, y2 = send(across2, "x"), send(side2, "y")
     x1, y1, _, _ = barrier((x1, y1, across2, side2))
     (up2,) = mix(mix_up, ids, [x1, y1], 1, 2 * 10**10)
     z2 = send(up2, "z")
+    carry = far(choose_first, devices_first, carry, [mate_k, mate_v], 0)
+    y2, z2, y1, x1, *carry = barrier((y2, z2, y1, x1, *carry))
     x1s, y1s = swap(x1, y1)
-    carry = far(choose_first, devices_first, carry, [mate_k, mate_v], 0)
-    y2, z2, y1, x1s, y1s, *carry = barrier((y2, z2, y1, x1s, y1s, *carry))
     x3 = send(y2, "x")
     side3, up3 = mix(mix_round3, ids, [x1, z2, y1, values], 2, 2 * 10**10)
     y3, z3 = send(side3, "y"), send(up3, "z")
@@ -315,7 +315,10 @@
     )
     x3, y3, z3, *carry = barrier((x3, y3, z3, *carry))
     z1s, x3s, y3s, z3s = swap(z1, x3, y3, z3)
-    carry = far(choose_last, functools.partial(devices_last, False), carry, [z1, y2, x3, y3, z3], 2 * rows)
+    carry = far(
+        choose_last, functools.partial(devices_last, False), carry, [z1, y2, x3, y3, z3], 2 * rows,
+        heads_step=2 * HEADS_STEP,
+    )
     (out,) = far(
         choose_last, functools.partial(devices_last, True), carry, [z1s, y2s, x3s, y3s, z3s], 2 * rows, True
     )

time: 64.5 us -> 62.4 us (0.967)
  starting transfers between devices: 11.8 us -> 10.7 us
  waiting for transfers between devices: 21.7 us -> 20.7 us
    ppermute x20, starting transfers between devices: 11.8 us -> 10.7 us  [send(): return lax.ppermute(array, AXES, along[way])]
    ppermute x20, waiting for transfers between devices: 21.7 us -> 20.7 us  [send(): return lax.ppermute(array, AXES, along[way])]
  transfers between devices with their start and end apart: 20 -> 20, of which waited for: 6 -> 6; matrix products, arithmetic and copies ran while one was open for 0% -> 0% of each run, Pallas kernels for 30% -> 32%
where the time goes in v2:
time: 62.4 us; the launch traced here: 61.4 us
  Pallas kernels  25.3 us (41%)
  waiting for transfers between devices  20.7 us (33%)
  starting transfers between devices  10.7 us (17%)
  local copies, waits for them, and re-layouts  4.27 us (7%)
    pallas_call x5, Pallas kernels, call(): pl.pallas_call(functools.partial(kernel, group), in_specs=[pl.BlockSpec(m...  23.4 us
    ppermute x20, waiting for transfers between devices, send(): return lax.ppermute(array, AXES, along[way])  20.7 us
    ppermute x20, starting transfers between devices, send(): return lax.ppermute(array, AXES, along[way])  10.7 us
    unnamed x16, local copies, waits for them, and re-layouts  4.27 us
    pallas_call x3, Pallas kernels, mix(): pl.pallas_call(functools.partial(mix_kernel, rule), in_specs=[pl.BlockSpe...  1.94 us
  transfers between devices with their start and end apart: 20, of which 6 were waited for; matrix products, arithmetic and copies ran while one was open for 0% of the time, Pallas kernels for 32%

profile of v2, /device:TPU:4, one launch (start us, length us, event | category | flops | bytes accessed | tf_op | source)
XLA Modules:
  0.0 61.4 jit_solution(18287701602602344447)
XLA Ops:
  0.0 1.6 %collective-permute-start = (bf16[256,1024]{1,0:T(8,128)(2,1)}, bf16[256,1024]{1,0:T(8,128)(2,1)S(1)}, u32[]{:S(2)}, u32[]{:S(2)}) collective-permute-start(bf16[256,1024]{1,0:T(8,128)(2,1)} %refs_0_.1), channel_id=1, source_target_pairs={{0,1},{1,0},{2,10},{3,11},{4,12},{5,13},{6,14},{7,15},{8,9},{9,8},... | collective-permute-start | bytes 1572872 | tf_op jit(solution)/shard_map/ppermute | solution.py:284
  1.6 1.5 %collective-permute-start.2 = (bf16[256,1024]{1,0:T(8,128)(2,1)}, bf16[256,1024]{1,0:T(8,128)(2,1)S(1)}, u32[]{:S(2)}, u32[]{:S(2)}) collective-permute-start(bf16[256,1024]{1,0:T(8,128)(2,1)} %refs_3_.1), channel_id=1, source_target_pairs={{0,2},{1,3},{2,0},{3,1},{4,6},{5,7},{6,4},{7,5},{8,10},{9,11},{10,... | collective-permute-start | bytes 1572872 | tf_op jit(solution)/shard_map/ppermute | solution.py:284
  3.1 0.5 collective-permute-start.3
  3.6 0.0 collective-permute-start.5
  3.6 0.5 collective-permute-start.6
  4.1 0.1 pad_add_fusion.ids
  4.2 0.0 copy-start
  4.2 1.4 %copy-done = bf16[256,3072]{1,0:T(8,128)(2,1)S(1)} copy-done((bf16[256,3072]{1,0:T(8,128)(2,1)S(1)}, bf16[256,3072]{1,0:T(8,128)(2,1)}, u32[]{:S(2)}) %copy-start) | copy-done | bytes 1572888
  5.6 0.0 copy-start.2
  5.6 0.8 %copy-done.2 = s32[8192]{0:T(1024)S(1)} copy-done((s32[8192]{0:T(1024)S(1)}, s32[8192]{0:T(1024)}, u32[]{:S(2)}) %copy-start.2) | copy-done | bytes 32792
  6.3 0.0 copy-start.4
  6.3 1.0 %copy-done.4 = bf16[256,1024]{1,0:T(8,128)(2,1)S(1)} copy-done((bf16[256,1024]{1,0:T(8,128)(2,1)S(1)}, bf16[256,1024]{1,0:T(8,128)(2,1)}, u32[]{:S(2)}) %copy-start.4) | copy-done | bytes 524312
  7.4 1.0 %copy-done.6 = bf16[256,1024]{1,0:T(8,128)(2,1)S(1)} copy-done((bf16[256,1024]{1,0:T(8,128)(2,1)S(1)}, bf16[256,1024]{1,0:T(8,128)(2,1)}, u32[]{:S(2)}) %copy-start.6) | copy-done | bytes 524312
  8.4 0.0 copy-start.5
  8.4 3.1 %shard_map.46 = (f32[256,3072]{1,0:T(8,128)S(1)}, f32[24,256,128]{2,1,0:T(8,128)S(1)}, f32[24,256,128]{2,1,0:T(8,128)S(1)}) custom-call(s32[3]{0:T(128)S(1)} %pad_add_fusion.ids, s32[64,128]{1,0:T(8,128)S(1)} %bitcast.3, bf16[256,3072]{1,0:T(8,128)(2,1)S(1)} %copy-done, bf16[256,1024]{1,0:T(8,128)(2,1)S(1)} %copy-done.4, bf16[256,1024]{1,0:T(8,128)(2,1)S(1)} %copy-done.6), custom_call_target="tpu_custom_call" | custom-call | flops 1610612736 | bytes 3145728 | tf_op jit(solution)/shard_map/pallas_call | solution.py:219
  11.5 4.2 %collective-permute-done.refs_1_.refs_0_ = bf16[256,1024]{1,0:T(8,128)(2,1)S(1)} collective-permute-done((bf16[256,1024]{1,0:T(8,128)(2,1)}, bf16[256,1024]{1,0:T(8,128)(2,1)S(1)}, u32[]{:S(2)}, u32[]{:S(2)}) %collective-permute-start) | collective-permute-done | bytes 524320 | tf_op jit(solution)/shard_map/ppermute | solution.py:284
  15.7 0.0 copy-done.5
  15.7 0.7 %shard_map.47 = (bf16[256,1024]{1,0:T(8,128)(2,1)S(1)}, bf16[256,1024]{1,0:T(8,128)(2,1)S(1)}) custom-call(s32[3]{0:T(128)S(1)} %pad_add_fusion.ids, bf16[256,1024]{1,0:T(8,128)(2,1)S(1)} %copy-done.5, bf16[256,1024]{1,0:T(8,128)(2,1)S(1)} %collective-permute-done.refs_1_.refs_0_), custom_call_target="tpu_custom_call" | custom-call | bytes 262144 | tf_op jit(solution)/shard_map/pallas_call | solution.py:239
  16.4 0.0 collective-permute-done.2.refs_0_
  16.4 0.0 collective-permute-done.3.refs_1_.refs_2_
  16.4 0.0 copy-start.1
  16.4 0.0 copy-start.3
  16.4 0.6 shard_map.48
  17.1 0.0 copy-start.7
  17.1 1.6 %collective-permute-start.4 = (bf16[256,1024]{1,0:T(8,128)(2,1)S(1)}, bf16[256,1024]{1,0:T(8,128)(2,1)S(1)}, u32[]{:S(2)}, u32[]{:S(2)}) collective-permute-start(bf16[256,1024]{1,0:T(8,128)(2,1)S(1)} %shard_map.48), channel_id=1, source_target_pairs={{0,8},{1,9},{2,10},{3,11},{4,12},{5,13},{6,14},{7,15},{8,16},{9,17... | collective-permute-start | bytes 1572872 | tf_op jit(solution)/shard_map/ppermute | solution.py:284
  18.6 0.5 collective-permute-start.1
  19.1 0.3 collective-permute-start.10
  19.5 0.0 collective-permute-done.5.refs_0_
  19.5 0.0 collective-permute-done.6.refs_1_
  19.5 0.0 copy-done.1
  19.5 0.0 copy-done.3
  19.5 1.6 %shard_map.49 = (f32[256,3072]{1,0:T(8,128)S(1)}, f32[24,256,128]{2,1,0:T(8,128)S(1)}, f32[24,256,128]{2,1,0:T(8,128)S(1)}) custom-call(s32[3]{0:T(128)S(1)} %pad_add_fusion.ids, s32[64,128]{1,0:T(8,128)S(1)} %bitcast.4, bf16[256,3072]{1,0:T(8,128)(2,1)S(1)} %copy-done.1, f32[256,3072]{1,0:T(8,128)S(1)} %get-tuple-element.48.acc_in, ...), custom_call_target="tpu_custom_call", output_to_operand_aliasing={{1}: (4, {})} | custom-call | tf_op jit(solution)/shard_map/pallas_call | solution.py:219
  21.1 10.7 %collective-permute-done.4.refs_1_.refs_4_ = bf16[256,1024]{1,0:T(8,128)(2,1)S(1)} collective-permute-done((bf16[256,1024]{1,0:T(8,128)(2,1)S(1)}, bf16[256,1024]{1,0:T(8,128)(2,1)S(1)}, u32[]{:S(2)}, u32[]{:S(2)}) %collective-permute-start.4) | collective-permute-done | bytes 524320 | tf_op jit(solution)/shard_map/ppermute | solution.py:284
  31.8 0.0 collective-permute-done.1.refs_3_.refs_1_
  31.8 0.0 collective-permute-start.11
  31.8 0.5 collective-permute-start.12
  32.3 0.0 collective-permute-start.14
  32.3 0.5 collective-permute-start.15
  32.8 0.0 copy-done.7
  32.8 0.7 %shard_map.50 = (bf16[256,1024]{1,0:T(8,128)(2,1)S(1)}, bf16[256,1024]{1,0:T(8,128)(2,1)S(1)}) custom-call(s32[3]{0:T(128)S(1)} %pad_add_fusion.ids, bf16[256,1024]{1,0:T(8,128)(2,1)S(1)} %collective-permute-done.2.refs_0_, bf16[256,1024]{1,0:T(8,128)(2,1)S(1)} %collective-permute-done.4.refs_1_.refs_4_, ...), custom_call_target="tpu_custom_call" | custom-call | flops 20000000000 | bytes 262144 | tf_op jit(solution)/shard_map/pallas_call | solution.py:239
  33.5 0.0 collective-permute-done.10.refs_2_
  33.5 0.1 collective-permute-start.13
  33.6 0.1 collective-permute-done.11.refs_5_
  33.7 0.8 %collective-permute-start.8 = (bf16[256,1024]{1,0:T(8,128)(2,1)S(1)}, bf16[256,1024]{1,0:T(8,128)(2,1)S(1)}, u32[]{:S(2)}, u32[]{:S(2)}) collective-permute-start(bf16[256,1024]{1,0:T(8,128)(2,1)S(1)} %get-tuple-element.58), channel_id=1, source_target_pairs={{0,4},{1,5},{2,6},{3,7},{4,0},{5,1},{6,2},{7,3},{8,12},{9,13},{10,... | collective-permute-start | bytes 1572872 | tf_op jit(solution)/shard_map/ppermute | solution.py:284
  34.5 0.0 collective-permute-done.12.refs_6_
  34.5 0.3 collective-permute-start.9
  34.8 0.4 collective-permute-done.14.refs_8_.refs_1_
  35.2 1.5 %collective-permute-start.7 = (bf16[256,1024]{1,0:T(8,128)(2,1)S(1)}, bf16[256,1024]{1,0:T(8,128)(2,1)S(1)}, u32[]{:S(2)}, u32[]{:S(2)}) collective-permute-start(bf16[256,1024]{1,0:T(8,128)(2,1)S(1)} %collective-permute-done.1.refs_3_.refs_1_), channel_id=1, source_target_pairs={{0,2},{1,3},{2,0},{3,1},{4,6},{5,7},{6,4},{7,5},{8,10},{9,11},{10,... | collective-permute-start | bytes 1572872 | tf_op jit(solution)/shard_map/ppermute | solution.py:284
  36.7 0.0 collective-permute-done.15.refs_9_
  36.7 0.0 collective-permute-start.16
  36.7 0.0 collective-permute-done.13.refs_7_
  36.7 8.3 %shard_map.51 = (f32[256,3072]{1,0:T(8,128)S(1)}, f32[24,256,128]{2,1,0:T(8,128)S(1)}, f32[24,256,128]{2,1,0:T(8,128)S(1)}) custom-call(s32[3]{0:T(128)S(1)} %pad_add_fusion.ids, s32[64,128]{1,0:T(8,128)S(1)} %bitcast.5, bf16[256,3072]{1,0:T(8,128)(2,1)S(1)} %copy-done.1, f32[256,3072]{1,0:T(8,128)S(1)} %get-tuple-element.60.acc_in, ...), custom_call_target="tpu_custom_call", output_to_operand_aliasing={{1}: (4, {})} | custom-call | tf_op jit(solution)/shard_map/pallas_call | solution.py:219
  45.0 2.9 %collective-permute-done.8.refs_3_ = bf16[256,1024]{1,0:T(8,128)(2,1)S(1)} collective-permute-done((bf16[256,1024]{1,0:T(8,128)(2,1)S(1)}, bf16[256,1024]{1,0:T(8,128)(2,1)S(1)}, u32[]{:S(2)}, u32[]{:S(2)}) %collective-permute-start.8) | collective-permute-done | bytes 524320 | tf_op jit(solution)/shard_map/ppermute | solution.py:284
  47.9 2.3 %collective-permute-done.9.refs_4_ = bf16[256,1024]{1,0:T(8,128)(2,1)S(1)} collective-permute-done((bf16[256,1024]{1,0:T(8,128)(2,1)S(1)}, bf16[256,1024]{1,0:T(8,128)(2,1)S(1)}, u32[]{:S(2)}, u32[]{:S(2)}) %collective-permute-start.9) | collective-permute-done | bytes 524320 | tf_op jit(solution)/shard_map/ppermute | solution.py:284
  50.2 0.0 collective-permute-done.7.refs_2_
  50.2 0.0 collective-permute-start.17
  50.2 0.5 collective-permute-start.18
  50.7 0.0 collective-permute-start.19
  50.7 4.6 %shard_map.52 = (f32[256,3072]{1,0:T(8,128)S(1)}, f32[24,256,128]{2,1,0:T(8,128)S(1)}, f32[24,256,128]{2,1,0:T(8,128)S(1)}) custom-call(s32[3]{0:T(128)S(1)} %pad_add_fusion.ids, s32[64,128]{1,0:T(8,128)S(1)} %bitcast.6, bf16[256,3072]{1,0:T(8,128)(2,1)S(1)} %copy-done.1, f32[256,3072]{1,0:T(8,128)S(1)} %get-tuple-element.66.acc_in, ...), custom_call_target="tpu_custom_call", output_to_operand_aliasing={{1}: (4, {})} | custom-call | flops 3221225472 | bytes 6291456 | tf_op jit(solution)/shard_map/pallas_call | solution.py:219
  55.4 0.0 collective-permute-done.16.refs_0_
  55.4 0.0 collective-permute-done.17.refs_2_
  55.4 0.0 collective-permute-done.18.refs_3_
  55.4 0.0 collective-permute-done.19.refs_4_
  55.4 5.8 %shard_map.53 = bf16[256,3072]{1,0:T(8,128)(2,1)} custom-call(s32[3]{0:T(128)S(1)} %pad_add_fusion.ids, s32[64,128]{1,0:T(8,128)S(1)} %bitcast.7, bf16[256,3072]{1,0:T(8,128)(2,1)S(1)} %copy-done.1, f32[256,3072]{1,0:T(8,128)S(1)} %get-tuple-element.72.acc_in, f32[24,256,128]{2,1,0:T(8,128)S(1)} %get-tuple-element.73.top_in, ...), custom_call_target="tpu_custom_call" | custom-call | flops 3221225472 | bytes 6291456 | tf_op jit(solution)/shard_map/pallas_call | solution.py:219
  (1 shorter events, 0.0 us)
Async XLA Ops:
  0.0 15.7 %collective-permute-start = (bf16[256,1024]{1,0:T(8,128)(2,1)}, bf16[256,1024]{1,0:T(8,128)(2,1)S(1)}, u32[]{:S(2)}, u32[]{:S(2)}) collective-permute-start(bf16[256,1024]{1,0:T(8,128)(2,1)} %refs_0_.1), channel_id=1, source_target_pairs={{0,1},{1,0},{2,10},{3,11},{4,12},{5,13},{6,14},{7,15},{8,9},{9,8},... | collective-permute-start | bytes 1572872 | tf_op jit(solution)/shard_map/ppermute | solution.py:284
  1.6 14.8 %collective-permute-start.2 = (bf16[256,1024]{1,0:T(8,128)(2,1)}, bf16[256,1024]{1,0:T(8,128)(2,1)S(1)}, u32[]{:S(2)}, u32[]{:S(2)}) collective-permute-start(bf16[256,1024]{1,0:T(8,128)(2,1)} %refs_3_.1), channel_id=1, source_target_pairs={{0,2},{1,3},{2,0},{3,1},{4,6},{5,7},{6,4},{7,5},{8,10},{9,11},{10,... | collective-permute-start | bytes 1572872 | tf_op jit(solution)/shard_map/ppermute | solution.py:284
  3.1 13.3 %collective-permute-start.3 = (bf16[256,1024]{1,0:T(8,128)(2,1)}, bf16[256,1024]{1,0:T(8,128)(2,1)S(1)}, u32[]{:S(2)}, u32[]{:S(2)}) collective-permute-start(bf16[256,1024]{1,0:T(8,128)(2,1)} %refs_3_.1), channel_id=1, source_target_pairs={{0,4},{1,5},{2,6},{3,7},{4,0},{5,1},{6,2},{7,3},{8,12},{9,13},{10,... | collective-permute-start | bytes 1572872 | tf_op jit(solution)/shard_map/ppermute | solution.py:284
  3.6 15.9 %collective-permute-start.5 = (bf16[256,1024]{1,0:T(8,128)(2,1)}, bf16[256,1024]{1,0:T(8,128)(2,1)S(1)}, u32[]{:S(2)}, u32[]{:S(2)}) collective-permute-start(bf16[256,1024]{1,0:T(8,128)(2,1)} %refs_0_.1), channel_id=1, source_target_pairs={{0,1},{1,8},{2,3},{3,2},{4,5},{5,4},{6,7},{7,6},{8,9},{9,16},{10,1... | collective-permute-start | bytes 1572872 | tf_op jit(solution)/shard_map/ppermute | solution.py:284
  3.6 15.9 %collective-permute-start.6 = (bf16[256,1024]{1,0:T(8,128)(2,1)}, bf16[256,1024]{1,0:T(8,128)(2,1)S(1)}, u32[]{:S(2)}, u32[]{:S(2)}) collective-permute-start(bf16[256,1024]{1,0:T(8,128)(2,1)} %refs_3_.1), channel_id=1, source_target_pairs={{0,1},{1,8},{2,3},{3,2},{4,5},{5,4},{6,7},{7,6},{8,9},{9,16},{10,1... | collective-permute-start | bytes 1572872 | tf_op jit(solution)/shard_map/ppermute | solution.py:284
  4.2 1.4 %copy-start = (bf16[256,3072]{1,0:T(8,128)(2,1)S(1)}, bf16[256,3072]{1,0:T(8,128)(2,1)}, u32[]{:S(2)}) copy-start(bf16[256,3072]{1,0:T(8,128)(2,1)} %q_ref.9) | copy-start | bytes 4718596
  5.6 0.8 %copy-start.2 = (s32[8192]{0:T(1024)S(1)}, s32[8192]{0:T(1024)}, u32[]{:S(2)}) copy-start(s32[8192]{0:T(1024)} %param.7) | copy-start | bytes 98308
  6.3 1.0 %copy-start.4 = (bf16[256,1024]{1,0:T(8,128)(2,1)S(1)}, bf16[256,1024]{1,0:T(8,128)(2,1)}, u32[]{:S(2)}) copy-start(bf16[256,1024]{1,0:T(8,128)(2,1)} %refs_0_.1) | copy-start | bytes 1572868
  7.4 1.0 %copy-start.6 = (bf16[256,1024]{1,0:T(8,128)(2,1)S(1)}, bf16[256,1024]{1,0:T(8,128)(2,1)}, u32[]{:S(2)}) copy-start(bf16[256,1024]{1,0:T(8,128)(2,1)} %refs_3_.1) | copy-start | bytes 1572868
  8.4 7.3 %copy-start.5 = (bf16[256,1024]{1,0:T(8,128)(2,1)S(1)}, bf16[256,1024]{1,0:T(8,128)(2,1)}, u32[]{:S(2)}) copy-start(bf16[256,1024]{1,0:T(8,128)(2,1)} %refs_0_.1) | copy-start | bytes 1572868
  16.4 3.1 %copy-start.1 = (bf16[256,3072]{1,0:T(8,128)(2,1)S(1)}, bf16[256,3072]{1,0:T(8,128)(2,1)}, u32[]{:S(2)}) copy-start(bf16[256,3072]{1,0:T(8,128)(2,1)} %q_ref.9) | copy-start | bytes 4718596
  16.4 3.1 %copy-start.3 = (s32[8192]{0:T(1024)S(1)}, s32[8192]{0:T(1024)}, u32[]{:S(2)}) copy-start(s32[8192]{0:T(1024)} %param.7) | copy-start | bytes 98308
  17.1 15.8 %copy-start.7 = (bf16[256,1024]{1,0:T(8,128)(2,1)S(1)}, bf16[256,1024]{1,0:T(8,128)(2,1)}, u32[]{:S(2)}) copy-start(bf16[256,1024]{1,0:T(8,128)(2,1)} %refs_3_.1) | copy-start | bytes 1572868
  17.1 14.7 %collective-permute-start.4 = (bf16[256,1024]{1,0:T(8,128)(2,1)S(1)}, bf16[256,1024]{1,0:T(8,128)(2,1)S(1)}, u32[]{:S(2)}, u32[]{:S(2)}) collective-permute-start(bf16[256,1024]{1,0:T(8,128)(2,1)S(1)} %shard_map.48), channel_id=1, source_target_pairs={{0,8},{1,9},{2,10},{3,11},{4,12},{5,13},{6,14},{7,15},{8,16},{9,17... | collective-permute-start | bytes 1572872 | tf_op jit(solution)/shard_map/ppermute | solution.py:284
  18.6 13.1 %collective-permute-start.1 = (bf16[256,1024]{1,0:T(8,128)(2,1)S(1)}, bf16[256,1024]{1,0:T(8,128)(2,1)S(1)}, u32[]{:S(2)}, u32[]{:S(2)}) collective-permute-start(bf16[256,1024]{1,0:T(8,128)(2,1)S(1)} %get-tuple-element.44), channel_id=1, source_target_pairs={{0,4},{1,5},{2,6},{3,7},{4,0},{5,1},{6,2},{7,3},{8,12},{9,13},{10,... | collective-permute-start | bytes 1572872 | tf_op jit(solution)/shard_map/ppermute | solution.py:284
  19.1 14.4 %collective-permute-start.10 = (bf16[256,1024]{1,0:T(8,128)(2,1)S(1)}, bf16[256,1024]{1,0:T(8,128)(2,1)S(1)}, u32[]{:S(2)}, u32[]{:S(2)}) collective-permute-start(bf16[256,1024]{1,0:T(8,128)(2,1)S(1)} %get-tuple-element.45), channel_id=1, source_target_pairs={{0,2},{1,3},{2,0},{3,1},{4,6},{5,7},{6,4},{7,5},{8,10},{9,11},{10,... | collective-permute-start | bytes 1572872 | tf_op jit(solution)/shard_map/ppermute | solution.py:284
  31.8 1.9 %collective-permute-start.11 = (bf16[256,1024]{1,0:T(8,128)(2,1)S(1)}, bf16[256,1024]{1,0:T(8,128)(2,1)S(1)}, u32[]{:S(2)}, u32[]{:S(2)}) collective-permute-start(bf16[256,1024]{1,0:T(8,128)(2,1)S(1)} %collective-permute-done.2.refs_0_), channel_id=1, source_target_pairs={{0,1},{1,0},{2,3},{3,2},{4,5},{5,4},{6,7},{7,6},{8,9},{9,8},{10,11... | collective-permute-start | bytes 1572872 | tf_op jit(solution)/shard_map/ppermute | solution.py:284
  31.8 2.7 %collective-permute-start.12 = (bf16[256,1024]{1,0:T(8,128)(2,1)S(1)}, bf16[256,1024]{1,0:T(8,128)(2,1)S(1)}, u32[]{:S(2)}, u32[]{:S(2)}) collective-permute-start(bf16[256,1024]{1,0:T(8,128)(2,1)S(1)} %collective-permute-done.3.refs_1_.refs_2_), channel_id=1, source_target_pairs={{0,1},{1,0},{2,3},{3,2},{4,5},{5,4},{6,7},{7,6},{8,9},{9,8},{10,11... | collective-permute-start | bytes 1572872 | tf_op jit(solution)/shard_map/ppermute | solution.py:284
  32.3 2.9 %collective-permute-start.14 = (bf16[256,1024]{1,0:T(8,128)(2,1)S(1)}, bf16[256,1024]{1,0:T(8,128)(2,1)S(1)}, u32[]{:S(2)}, u32[]{:S(2)}) collective-permute-start(bf16[256,1024]{1,0:T(8,128)(2,1)S(1)} %collective-permute-done.1.refs_3_.refs_1_), channel_id=1, source_target_pairs={{0,1},{1,0},{2,3},{3,2},{4,5},{5,4},{6,7},{7,6},{8,9},{9,8},{10,11... | collective-permute-start | bytes 1572872 | tf_op jit(solution)/shard_map/ppermute | solution.py:284
  32.3 4.4 %collective-permute-start.15 = (bf16[256,1024]{1,0:T(8,128)(2,1)S(1)}, bf16[256,1024]{1,0:T(8,128)(2,1)S(1)}, u32[]{:S(2)}, u32[]{:S(2)}) collective-permute-start(bf16[256,1024]{1,0:T(8,128)(2,1)S(1)} %collective-permute-done.4.refs_1_.refs_4_), channel_id=1, source_target_pairs={{0,1},{1,0},{2,3},{3,2},{4,5},{5,4},{6,7},{7,6},{8,9},{9,8},{10,11... | collective-permute-start | bytes 1572872 | tf_op jit(solution)/shard_map/ppermute | solution.py:284
  33.5 3.2 %collective-permute-start.13 = (bf16[256,1024]{1,0:T(8,128)(2,1)S(1)}, bf16[256,1024]{1,0:T(8,128)(2,1)S(1)}, u32[]{:S(2)}, u32[]{:S(2)}) collective-permute-start(bf16[256,1024]{1,0:T(8,128)(2,1)S(1)} %collective-permute-done.10.refs_2_), channel_id=1, source_target_pairs={{0,1},{1,0},{2,3},{3,2},{4,5},{5,4},{6,7},{7,6},{8,9},{9,8},{10,11... | collective-permute-start | bytes 1572872 | tf_op jit(solution)/shard_map/ppermute | solution.py:284
  33.7 14.2 %collective-permute-start.8 = (bf16[256,1024]{1,0:T(8,128)(2,1)S(1)}, bf16[256,1024]{1,0:T(8,128)(2,1)S(1)}, u32[]{:S(2)}, u32[]{:S(2)}) collective-permute-start(bf16[256,1024]{1,0:T(8,128)(2,1)S(1)} %get-tuple-element.58), channel_id=1, source_target_pairs={{0,4},{1,5},{2,6},{3,7},{4,0},{5,1},{6,2},{7,3},{8,12},{9,13},{10,... | collective-permute-start | bytes 1572872 | tf_op jit(solution)/shard_map/ppermute | solution.py:284
  34.5 15.7 %collective-permute-start.9 = (bf16[256,1024]{1,0:T(8,128)(2,1)S(1)}, bf16[256,1024]{1,0:T(8,128)(2,1)S(1)}, u32[]{:S(2)}, u32[]{:S(2)}) collective-permute-start(bf16[256,1024]{1,0:T(8,128)(2,1)S(1)} %get-tuple-element.59), channel_id=1, source_target_pairs={{0,8},{1,9},{2,10},{3,11},{4,12},{5,13},{6,14},{7,15},{8,16},{9,17... | collective-permute-start | bytes 1572872 | tf_op jit(solution)/shard_map/ppermute | solution.py:284
  35.2 15.0 %collective-permute-start.7 = (bf16[256,1024]{1,0:T(8,128)(2,1)S(1)}, bf16[256,1024]{1,0:T(8,128)(2,1)S(1)}, u32[]{:S(2)}, u32[]{:S(2)}) collective-permute-start(bf16[256,1024]{1,0:T(8,128)(2,1)S(1)} %collective-permute-done.1.refs_3_.refs_1_), channel_id=1, source_target_pairs={{0,2},{1,3},{2,0},{3,1},{4,6},{5,7},{6,4},{7,5},{8,10},{9,11},{10,... | collective-permute-start | bytes 1572872 | tf_op jit(solution)/shard_map/ppermute | solution.py:284
  36.7 18.7 %collective-permute-start.16 = (bf16[256,1024]{1,0:T(8,128)(2,1)S(1)}, bf16[256,1024]{1,0:T(8,128)(2,1)S(1)}, u32[]{:S(2)}, u32[]{:S(2)}) collective-permute-start(bf16[256,1024]{1,0:T(8,128)(2,1)S(1)} %collective-permute-done.refs_1_.refs_0_), channel_id=1, source_target_pairs={{0,1},{1,0},{2,3},{3,2},{4,5},{5,4},{6,7},{7,6},{8,9},{9,8},{10,11... | collective-permute-start | bytes 1572872 | tf_op jit(solution)/shard_map/ppermute | solution.py:284
  50.2 5.2 %collective-permute-start.17 = (bf16[256,1024]{1,0:T(8,128)(2,1)S(1)}, bf16[256,1024]{1,0:T(8,128)(2,1)S(1)}, u32[]{:S(2)}, u32[]{:S(2)}) collective-permute-start(bf16[256,1024]{1,0:T(8,128)(2,1)S(1)} %collective-permute-done.7.refs_2_), channel_id=1, source_target_pairs={{0,1},{1,0},{2,3},{3,2},{4,5},{5,4},{6,7},{7,6},{8,9},{9,8},{10,11... | collective-permute-start | bytes 1572872 | tf_op jit(solution)/shard_map/ppermute | solution.py:284
  50.2 5.2 %collective-permute-start.18 = (bf16[256,1024]{1,0:T(8,128)(2,1)S(1)}, bf16[256,1024]{1,0:T(8,128)(2,1)S(1)}, u32[]{:S(2)}, u32[]{:S(2)}) collective-permute-start(bf16[256,1024]{1,0:T(8,128)(2,1)S(1)} %collective-permute-done.8.refs_3_), channel_id=1, source_target_pairs={{0,1},{1,0},{2,3},{3,2},{4,5},{5,4},{6,7},{7,6},{8,9},{9,8},{10,11... | collective-permute-start | bytes 1572872 | tf_op jit(solution)/shard_map/ppermute | solution.py:284
  50.7 4.7 %collective-permute-start.19 = (bf16[256,1024]{1,0:T(8,128)(2,1)S(1)}, bf16[256,1024]{1,0:T(8,128)(2,1)S(1)}, u32[]{:S(2)}, u32[]{:S(2)}) collective-permute-start(bf16[256,1024]{1,0:T(8,128)(2,1)S(1)} %collective-permute-done.9.refs_4_), channel_id=1, source_target_pairs={{0,1},{1,0},{2,3},{3,2},{4,5},{5,4},{6,7},{7,6},{8,9},{9,8},{10,11... | collective-permute-start | bytes 1572872 | tf_op jit(solution)/shard_map/ppermute | solution.py:284

commit v3 on v2

--- a/solution.py
+++ b/solution.py
@@ -304,8 +304,9 @@
     (up2,) = mix(mix_up, ids, [x1, y1], 1, 2 * 10**10)
     z2 = send(up2, "z")
     carry = far(choose_first, devices_first, carry, [mate_k, mate_v], 0)
+    x1, y1, *carry = barrier((x1, y1, *carry))
+    x1s, y1s = swap(x1, y1)
     y2, z2, y1, x1, *carry = barrier((y2, z2, y1, x1, *carry))
-    x1s, y1s = swap(x1, y1)
     x3 = send(y2, "x")
     side3, up3 = mix(mix_round3, ids, [x1, z2, y1, values], 2, 2 * 10**10)
     y3, z3 = send(side3, "y"), send(up3, "z")

time: 62.4 us -> 60.5 us (0.970)
  the two profiles are of different devices: /device:TPU:4 before, /device:TPU:24 now
where the time goes in v3:
time: 60.5 us; the launch traced here: 59.8 us
  waiting for transfers between devices  20.1 us (33%)
  Pallas kernels  18.6 us (31%)
  starting transfers between devices  16.4 us (27%)
  local copies, waits for them, and re-layouts  4.27 us (7%)
    ppermute x20, waiting for transfers between devices, send(): return lax.ppermute(array, AXES, along[way])  20.1 us
    pallas_call x5, Pallas kernels, call(): pl.pallas_call(functools.partial(kernel, group), in_specs=[pl.BlockSpec(m...  16.7 us
    ppermute x20, starting transfers between devices, send(): return lax.ppermute(array, AXES, along[way])  16.4 us
    unnamed x16, local copies, waits for them, and re-layouts  4.27 us
    pallas_call x3, Pallas kernels, mix(): pl.pallas_call(functools.partial(mix_kernel, rule), in_specs=[pl.BlockSpe...  1.94 us
  transfers between devices with their start and end apart: 20, of which 8 were waited for; matrix products, arithmetic and copies ran while one was open for 0% of the time, Pallas kernels for 22%

profile of v3, /device:TPU:24, one launch (start us, length us, event | category | flops | bytes accessed | tf_op | source)
XLA Modules:
  0.0 59.8 jit_solution(8042137491981339330)
XLA Ops:
  0.0 0.0 collective-permute-start
  0.0 1.7 %collective-permute-start.2 = (bf16[256,1024]{1,0:T(8,128)(2,1)}, bf16[256,1024]{1,0:T(8,128)(2,1)S(1)}, u32[]{:S(2)}, u32[]{:S(2)}) collective-permute-start(bf16[256,1024]{1,0:T(8,128)(2,1)} %refs_3_.1), channel_id=1, source_target_pairs={{0,2},{1,3},{2,0},{3,1},{4,6},{5,7},{6,4},{7,5},{8,10},{9,11},{10,... | collective-permute-start | bytes 1572872 | tf_op jit(solution)/shard_map/ppermute | solution.py:284
  1.7 1.5 %collective-permute-start.3 = (bf16[256,1024]{1,0:T(8,128)(2,1)}, bf16[256,1024]{1,0:T(8,128)(2,1)S(1)}, u32[]{:S(2)}, u32[]{:S(2)}) collective-permute-start(bf16[256,1024]{1,0:T(8,128)(2,1)} %refs_3_.1), channel_id=1, source_target_pairs={{0,4},{1,5},{2,6},{3,7},{4,0},{5,1},{6,2},{7,3},{8,12},{9,13},{10,... | collective-permute-start | bytes 1572872 | tf_op jit(solution)/shard_map/ppermute | solution.py:284
  3.2 0.0 collective-permute-start.5
  3.2 1.7 %collective-permute-start.6 = (bf16[256,1024]{1,0:T(8,128)(2,1)}, bf16[256,1024]{1,0:T(8,128)(2,1)S(1)}, u32[]{:S(2)}, u32[]{:S(2)}) collective-permute-start(bf16[256,1024]{1,0:T(8,128)(2,1)} %refs_3_.1), channel_id=1, source_target_pairs={{0,1},{1,8},{2,3},{3,2},{4,5},{5,4},{6,7},{7,6},{8,9},{9,16},{10,1... | collective-permute-start | bytes 1572872 | tf_op jit(solution)/shard_map/ppermute | solution.py:284
  4.9 0.1 pad_add_fusion.ids
  5.0 0.0 copy-start
  5.0 1.4 %copy-done = bf16[256,3072]{1,0:T(8,128)(2,1)S(1)} copy-done((bf16[256,3072]{1,0:T(8,128)(2,1)S(1)}, bf16[256,3072]{1,0:T(8,128)(2,1)}, u32[]{:S(2)}) %copy-start) | copy-done | bytes 1572888
  6.4 0.0 copy-start.2
  6.4 0.8 %copy-done.2 = s32[8192]{0:T(1024)S(1)} copy-done((s32[8192]{0:T(1024)S(1)}, s32[8192]{0:T(1024)}, u32[]{:S(2)}) %copy-start.2) | copy-done | bytes 32792
  7.2 0.0 copy-start.4
  7.2 1.0 %copy-done.4 = bf16[256,1024]{1,0:T(8,128)(2,1)S(1)} copy-done((bf16[256,1024]{1,0:T(8,128)(2,1)S(1)}, bf16[256,1024]{1,0:T(8,128)(2,1)}, u32[]{:S(2)}) %copy-start.4) | copy-done | bytes 524312
  8.2 0.0 copy-start.6
  8.2 1.0 %copy-done.6 = bf16[256,1024]{1,0:T(8,128)(2,1)S(1)} copy-done((bf16[256,1024]{1,0:T(8,128)(2,1)S(1)}, bf16[256,1024]{1,0:T(8,128)(2,1)}, u32[]{:S(2)}) %copy-start.6) | copy-done | bytes 524312
  9.3 0.0 copy-start.5
  9.3 3.1 %shard_map.46 = (f32[256,3072]{1,0:T(8,128)S(1)}, f32[24,256,128]{2,1,0:T(8,128)S(1)}, f32[24,256,128]{2,1,0:T(8,128)S(1)}) custom-call(s32[3]{0:T(128)S(1)} %pad_add_fusion.ids, s32[64,128]{1,0:T(8,128)S(1)} %bitcast.3, bf16[256,3072]{1,0:T(8,128)(2,1)S(1)} %copy-done, bf16[256,1024]{1,0:T(8,128)(2,1)S(1)} %copy-done.4, bf16[256,1024]{1,0:T(8,128)(2,1)S(1)} %copy-done.6), custom_call_target="tpu_custom_call" | custom-call | flops 1610612736 | bytes 3145728 | tf_op jit(solution)/shard_map/pallas_call | solution.py:219
  12.4 0.0 collective-permute-done.refs_1_.refs_0_
  12.4 0.0 copy-done.5
  12.4 0.7 %shard_map.47 = (bf16[256,1024]{1,0:T(8,128)(2,1)S(1)}, bf16[256,1024]{1,0:T(8,128)(2,1)S(1)}) custom-call(s32[3]{0:T(128)S(1)} %pad_add_fusion.ids, bf16[256,1024]{1,0:T(8,128)(2,1)S(1)} %copy-done.5, bf16[256,1024]{1,0:T(8,128)(2,1)S(1)} %collective-permute-done.refs_1_.refs_0_), custom_call_target="tpu_custom_call" | custom-call | bytes 262144 | tf_op jit(solution)/shard_map/pallas_call | solution.py:239
  13.1 1.5 %collective-permute-done.2.refs_0_ = bf16[256,1024]{1,0:T(8,128)(2,1)S(1)} collective-permute-done((bf16[256,1024]{1,0:T(8,128)(2,1)}, bf16[256,1024]{1,0:T(8,128)(2,1)S(1)}, u32[]{:S(2)}, u32[]{:S(2)}) %collective-permute-start.2) | collective-permute-done | bytes 524320 | tf_op jit(solution)/shard_map/ppermute | solution.py:284
  14.6 0.5 collective-permute-done.3.refs_1_.refs_2_
  15.1 0.0 copy-start.1
  15.1 0.6 shard_map.48
  15.7 0.0 copy-start.7
  15.7 1.6 %collective-permute-start.4 = (bf16[256,1024]{1,0:T(8,128)(2,1)S(1)}, bf16[256,1024]{1,0:T(8,128)(2,1)S(1)}, u32[]{:S(2)}, u32[]{:S(2)}) collective-permute-start(bf16[256,1024]{1,0:T(8,128)(2,1)S(1)} %shard_map.48), channel_id=1, source_target_pairs={{0,8},{1,9},{2,10},{3,11},{4,12},{5,13},{6,14},{7,15},{8,16},{9,17... | collective-permute-start | bytes 1572872 | tf_op jit(solution)/shard_map/ppermute | solution.py:284
  17.3 1.6 %collective-permute-start.1 = (bf16[256,1024]{1,0:T(8,128)(2,1)S(1)}, bf16[256,1024]{1,0:T(8,128)(2,1)S(1)}, u32[]{:S(2)}, u32[]{:S(2)}) collective-permute-start(bf16[256,1024]{1,0:T(8,128)(2,1)S(1)} %get-tuple-element.49), channel_id=1, source_target_pairs={{0,4},{1,5},{2,6},{3,7},{4,0},{5,1},{6,2},{7,3},{8,12},{9,13},{10,... | collective-permute-start | bytes 1572872 | tf_op jit(solution)/shard_map/ppermute | solution.py:284
  18.9 1.5 %collective-permute-start.10 = (bf16[256,1024]{1,0:T(8,128)(2,1)S(1)}, bf16[256,1024]{1,0:T(8,128)(2,1)S(1)}, u32[]{:S(2)}, u32[]{:S(2)}) collective-permute-start(bf16[256,1024]{1,0:T(8,128)(2,1)S(1)} %get-tuple-element.50), channel_id=1, source_target_pairs={{0,2},{1,3},{2,0},{3,1},{4,6},{5,7},{6,4},{7,5},{8,10},{9,11},{10,... | collective-permute-start | bytes 1572872 | tf_op jit(solution)/shard_map/ppermute | solution.py:284
  20.3 0.0 collective-permute-done.5.refs_0_
  20.4 0.0 collective-permute-done.6.refs_1_
  20.4 0.0 copy-done.1
  20.4 0.0 copy-done.3
  20.4 1.6 %shard_map.49 = (f32[256,3072]{1,0:T(8,128)S(1)}, f32[24,256,128]{2,1,0:T(8,128)S(1)}, f32[24,256,128]{2,1,0:T(8,128)S(1)}) custom-call(s32[3]{0:T(128)S(1)} %pad_add_fusion.ids, s32[64,128]{1,0:T(8,128)S(1)} %bitcast.4, bf16[256,3072]{1,0:T(8,128)(2,1)S(1)} %copy-done.1, f32[256,3072]{1,0:T(8,128)S(1)} %get-tuple-element.53.acc_in, ...), custom_call_target="tpu_custom_call", output_to_operand_aliasing={{1}: (4, {})} | custom-call | tf_op jit(solution)/shard_map/pallas_call | solution.py:219
  22.0 0.1 collective-permute-start.11
  22.0 0.5 collective-permute-start.12
  22.5 6.4 %collective-permute-done.4.refs_1_.refs_4_ = bf16[256,1024]{1,0:T(8,128)(2,1)S(1)} collective-permute-done((bf16[256,1024]{1,0:T(8,128)(2,1)S(1)}, bf16[256,1024]{1,0:T(8,128)(2,1)S(1)}, u32[]{:S(2)}, u32[]{:S(2)}) %collective-permute-start.4) | collective-permute-done | bytes 524320 | tf_op jit(solution)/shard_map/ppermute | solution.py:284
  28.9 0.8 %collective-permute-done.1.refs_3_.refs_1_ = bf16[256,1024]{1,0:T(8,128)(2,1)S(1)} collective-permute-done((bf16[256,1024]{1,0:T(8,128)(2,1)S(1)}, bf16[256,1024]{1,0:T(8,128)(2,1)S(1)}, u32[]{:S(2)}, u32[]{:S(2)}) %collective-permute-start.1) | collective-permute-done | bytes 524320 | tf_op jit(solution)/shard_map/ppermute | solution.py:284
  29.7 0.0 collective-permute-start.14
  29.7 0.5 collective-permute-start.15
  30.2 0.0 copy-done.7
  30.2 0.7 %shard_map.50 = (bf16[256,1024]{1,0:T(8,128)(2,1)S(1)}, bf16[256,1024]{1,0:T(8,128)(2,1)S(1)}) custom-call(s32[3]{0:T(128)S(1)} %pad_add_fusion.ids, bf16[256,1024]{1,0:T(8,128)(2,1)S(1)} %collective-permute-done.2.refs_0_, bf16[256,1024]{1,0:T(8,128)(2,1)S(1)} %collective-permute-done.4.refs_1_.refs_4_, ...), custom_call_target="tpu_custom_call" | custom-call | flops 20000000000 | bytes 262144 | tf_op jit(solution)/shard_map/pallas_call | solution.py:239
  30.9 0.3 collective-permute-done.10.refs_2_
  31.2 0.0 collective-permute-start.13
  31.2 0.0 collective-permute-done.11.refs_5_
  31.2 1.6 %collective-permute-start.8 = (bf16[256,1024]{1,0:T(8,128)(2,1)S(1)}, bf16[256,1024]{1,0:T(8,128)(2,1)S(1)}, u32[]{:S(2)}, u32[]{:S(2)}) collective-permute-start(bf16[256,1024]{1,0:T(8,128)(2,1)S(1)} %get-tuple-element.68), channel_id=1, source_target_pairs={{0,4},{1,5},{2,6},{3,7},{4,0},{5,1},{6,2},{7,3},{8,12},{9,13},{10,... | collective-permute-start | bytes 1572872 | tf_op jit(solution)/shard_map/ppermute | solution.py:284
  32.8 0.0 collective-permute-done.12.refs_6_
  32.8 2.1 %collective-permute-start.9 = (bf16[256,1024]{1,0:T(8,128)(2,1)S(1)}, bf16[256,1024]{1,0:T(8,128)(2,1)S(1)}, u32[]{:S(2)}, u32[]{:S(2)}) collective-permute-start(bf16[256,1024]{1,0:T(8,128)(2,1)S(1)} %get-tuple-element.69), channel_id=1, source_target_pairs={{0,8},{1,9},{2,10},{3,11},{4,12},{5,13},{6,14},{7,15},{8,16},{9,17... | collective-permute-start | bytes 1572872 | tf_op jit(solution)/shard_map/ppermute | solution.py:284
  34.9 0.0 collective-permute-done.14.refs_8_.refs_1_
  34.9 1.5 %collective-permute-start.7 = (bf16[256,1024]{1,0:T(8,128)(2,1)S(1)}, bf16[256,1024]{1,0:T(8,128)(2,1)S(1)}, u32[]{:S(2)}, u32[]{:S(2)}) collective-permute-start(bf16[256,1024]{1,0:T(8,128)(2,1)S(1)} %collective-permute-done.1.refs_3_.refs_1_), channel_id=1, source_target_pairs={{0,2},{1,3},{2,0},{3,1},{4,6},{5,7},{6,4},{7,5},{8,10},{9,11},{10,... | collective-permute-start | bytes 1572872 | tf_op jit(solution)/shard_map/ppermute | solution.py:284
  36.4 0.0 collective-permute-done.15.refs_9_
  36.4 0.0 collective-permute-start.16
  36.4 0.0 collective-permute-done.13.refs_7_
  36.4 1.6 %shard_map.51 = (f32[256,3072]{1,0:T(8,128)S(1)}, f32[24,256,128]{2,1,0:T(8,128)S(1)}, f32[24,256,128]{2,1,0:T(8,128)S(1)}) custom-call(s32[3]{0:T(128)S(1)} %pad_add_fusion.ids, s32[64,128]{1,0:T(8,128)S(1)} %bitcast.5, bf16[256,3072]{1,0:T(8,128)(2,1)S(1)} %copy-done.1, f32[256,3072]{1,0:T(8,128)S(1)} %get-tuple-element.70.acc_in, ...), custom_call_target="tpu_custom_call", output_to_operand_aliasing={{1}: (4, {})} | custom-call | tf_op jit(solution)/shard_map/pallas_call | solution.py:219
  38.0 7.5 %collective-permute-done.8.refs_3_ = bf16[256,1024]{1,0:T(8,128)(2,1)S(1)} collective-permute-done((bf16[256,1024]{1,0:T(8,128)(2,1)S(1)}, bf16[256,1024]{1,0:T(8,128)(2,1)S(1)}, u32[]{:S(2)}, u32[]{:S(2)}) %collective-permute-start.8) | collective-permute-done | bytes 524320 | tf_op jit(solution)/shard_map/ppermute | solution.py:284
  45.5 1.3 %collective-permute-done.9.refs_4_ = bf16[256,1024]{1,0:T(8,128)(2,1)S(1)} collective-permute-done((bf16[256,1024]{1,0:T(8,128)(2,1)S(1)}, bf16[256,1024]{1,0:T(8,128)(2,1)S(1)}, u32[]{:S(2)}, u32[]{:S(2)}) %collective-permute-start.9) | collective-permute-done | bytes 524320 | tf_op jit(solution)/shard_map/ppermute | solution.py:284
  46.8 1.8 %collective-permute-done.7.refs_2_ = bf16[256,1024]{1,0:T(8,128)(2,1)S(1)} collective-permute-done((bf16[256,1024]{1,0:T(8,128)(2,1)S(1)}, bf16[256,1024]{1,0:T(8,128)(2,1)S(1)}, u32[]{:S(2)}, u32[]{:S(2)}) %collective-permute-start.7) | collective-permute-done | bytes 524320 | tf_op jit(solution)/shard_map/ppermute | solution.py:284
  48.6 0.0 collective-permute-start.17
  48.6 0.5 collective-permute-start.18
  49.1 0.0 collective-permute-start.19
  49.1 4.6 %shard_map.52 = (f32[256,3072]{1,0:T(8,128)S(1)}, f32[24,256,128]{2,1,0:T(8,128)S(1)}, f32[24,256,128]{2,1,0:T(8,128)S(1)}) custom-call(s32[3]{0:T(128)S(1)} %pad_add_fusion.ids, s32[64,128]{1,0:T(8,128)S(1)} %bitcast.6, bf16[256,3072]{1,0:T(8,128)(2,1)S(1)} %copy-done.1, f32[256,3072]{1,0:T(8,128)S(1)} %get-tuple-element.76.acc_in, ...), custom_call_target="tpu_custom_call", output_to_operand_aliasing={{1}: (4, {})} | custom-call | flops 3221225472 | bytes 6291456 | tf_op jit(solution)/shard_map/pallas_call | solution.py:219
  53.8 0.0 collective-permute-done.16.refs_0_
  53.8 0.0 collective-permute-done.17.refs_2_
  53.8 0.0 collective-permute-done.18.refs_3_
  53.8 0.0 collective-permute-done.19.refs_4_
  53.8 5.8 %shard_map.53 = bf16[256,3072]{1,0:T(8,128)(2,1)} custom-call(s32[3]{0:T(128)S(1)} %pad_add_fusion.ids, s32[64,128]{1,0:T(8,128)S(1)} %bitcast.7, bf16[256,3072]{1,0:T(8,128)(2,1)S(1)} %copy-done.1, f32[256,3072]{1,0:T(8,128)S(1)} %get-tuple-element.82.acc_in, f32[24,256,128]{2,1,0:T(8,128)S(1)} %get-tuple-element.83.top_in, ...), custom_call_target="tpu_custom_call" | custom-call | flops 3221225472 | bytes 6291456 | tf_op jit(solution)/shard_map/pallas_call | solution.py:219
  (1 shorter events, 0.0 us)
Async XLA Ops:
  0.0 12.4 %collective-permute-start = (bf16[256,1024]{1,0:T(8,128)(2,1)}, bf16[256,1024]{1,0:T(8,128)(2,1)S(1)}, u32[]{:S(2)}, u32[]{:S(2)}) collective-permute-start(bf16[256,1024]{1,0:T(8,128)(2,1)} %refs_0_.1), channel_id=1, source_target_pairs={{0,1},{1,0},{2,10},{3,11},{4,12},{5,13},{6,14},{7,15},{8,9},{9,8},... | collective-permute-start | bytes 1572872 | tf_op jit(solution)/shard_map/ppermute | solution.py:284
  0.0 14.5 %collective-permute-start.2 = (bf16[256,1024]{1,0:T(8,128)(2,1)}, bf16[256,1024]{1,0:T(8,128)(2,1)S(1)}, u32[]{:S(2)}, u32[]{:S(2)}) collective-permute-start(bf16[256,1024]{1,0:T(8,128)(2,1)} %refs_3_.1), channel_id=1, source_target_pairs={{0,2},{1,3},{2,0},{3,1},{4,6},{5,7},{6,4},{7,5},{8,10},{9,11},{10,... | collective-permute-start | bytes 1572872 | tf_op jit(solution)/shard_map/ppermute | solution.py:284
  1.7 13.4 %collective-permute-start.3 = (bf16[256,1024]{1,0:T(8,128)(2,1)}, bf16[256,1024]{1,0:T(8,128)(2,1)S(1)}, u32[]{:S(2)}, u32[]{:S(2)}) collective-permute-start(bf16[256,1024]{1,0:T(8,128)(2,1)} %refs_3_.1), channel_id=1, source_target_pairs={{0,4},{1,5},{2,6},{3,7},{4,0},{5,1},{6,2},{7,3},{8,12},{9,13},{10,... | collective-permute-start | bytes 1572872 | tf_op jit(solution)/shard_map/ppermute | solution.py:284
  3.2 17.1 %collective-permute-start.5 = (bf16[256,1024]{1,0:T(8,128)(2,1)}, bf16[256,1024]{1,0:T(8,128)(2,1)S(1)}, u32[]{:S(2)}, u32[]{:S(2)}) collective-permute-start(bf16[256,1024]{1,0:T(8,128)(2,1)} %refs_0_.1), channel_id=1, source_target_pairs={{0,1},{1,8},{2,3},{3,2},{4,5},{5,4},{6,7},{7,6},{8,9},{9,16},{10,1... | collective-permute-start | bytes 1572872 | tf_op jit(solution)/shard_map/ppermute | solution.py:284
  3.2 17.1 %collective-permute-start.6 = (bf16[256,1024]{1,0:T(8,128)(2,1)}, bf16[256,1024]{1,0:T(8,128)(2,1)S(1)}, u32[]{:S(2)}, u32[]{:S(2)}) collective-permute-start(bf16[256,1024]{1,0:T(8,128)(2,1)} %refs_3_.1), channel_id=1, source_target_pairs={{0,1},{1,8},{2,3},{3,2},{4,5},{5,4},{6,7},{7,6},{8,9},{9,16},{10,1... | collective-permute-start | bytes 1572872 | tf_op jit(solution)/shard_map/ppermute | solution.py:284
  5.0 1.4 %copy-start = (bf16[256,3072]{1,0:T(8,128)(2,1)S(1)}, bf16[256,3072]{1,0:T(8,128)(2,1)}, u32[]{:S(2)}) copy-start(bf16[256,3072]{1,0:T(8,128)(2,1)} %q_ref.9) | copy-start | bytes 4718596
  6.4 0.8 %copy-start.2 = (s32[8192]{0:T(1024)S(1)}, s32[8192]{0:T(1024)}, u32[]{:S(2)}) copy-start(s32[8192]{0:T(1024)} %param.7) | copy-start | bytes 98308
  7.2 1.0 %copy-start.4 = (bf16[256,1024]{1,0:T(8,128)(2,1)S(1)}, bf16[256,1024]{1,0:T(8,128)(2,1)}, u32[]{:S(2)}) copy-start(bf16[256,1024]{1,0:T(8,128)(2,1)} %refs_0_.1) | copy-start | bytes 1572868
  8.2 1.0 %copy-start.6 = (bf16[256,1024]{1,0:T(8,128)(2,1)S(1)}, bf16[256,1024]{1,0:T(8,128)(2,1)}, u32[]{:S(2)}) copy-start(bf16[256,1024]{1,0:T(8,128)(2,1)} %refs_3_.1) | copy-start | bytes 1572868
  9.3 3.1 %copy-start.5 = (bf16[256,1024]{1,0:T(8,128)(2,1)S(1)}, bf16[256,1024]{1,0:T(8,128)(2,1)}, u32[]{:S(2)}) copy-start(bf16[256,1024]{1,0:T(8,128)(2,1)} %refs_0_.1) | copy-start | bytes 1572868
  15.1 5.3 %copy-start.1 = (bf16[256,3072]{1,0:T(8,128)(2,1)S(1)}, bf16[256,3072]{1,0:T(8,128)(2,1)}, u32[]{:S(2)}) copy-start(bf16[256,3072]{1,0:T(8,128)(2,1)} %q_ref.9) | copy-start | bytes 4718596
  15.1 5.3 %copy-start.3 = (s32[8192]{0:T(1024)S(1)}, s32[8192]{0:T(1024)}, u32[]{:S(2)}) copy-start(s32[8192]{0:T(1024)} %param.7) | copy-start | bytes 98308
  15.7 14.5 %copy-start.7 = (bf16[256,1024]{1,0:T(8,128)(2,1)S(1)}, bf16[256,1024]{1,0:T(8,128)(2,1)}, u32[]{:S(2)}) copy-start(bf16[256,1024]{1,0:T(8,128)(2,1)} %refs_3_.1) | copy-start | bytes 1572868
  15.7 13.2 %collective-permute-start.4 = (bf16[256,1024]{1,0:T(8,128)(2,1)S(1)}, bf16[256,1024]{1,0:T(8,128)(2,1)S(1)}, u32[]{:S(2)}, u32[]{:S(2)}) collective-permute-start(bf16[256,1024]{1,0:T(8,128)(2,1)S(1)} %shard_map.48), channel_id=1, source_target_pairs={{0,8},{1,9},{2,10},{3,11},{4,12},{5,13},{6,14},{7,15},{8,16},{9,17... | collective-permute-start | bytes 1572872 | tf_op jit(solution)/shard_map/ppermute | solution.py:284
  17.3 12.4 %collective-permute-start.1 = (bf16[256,1024]{1,0:T(8,128)(2,1)S(1)}, bf16[256,1024]{1,0:T(8,128)(2,1)S(1)}, u32[]{:S(2)}, u32[]{:S(2)}) collective-permute-start(bf16[256,1024]{1,0:T(8,128)(2,1)S(1)} %get-tuple-element.49), channel_id=1, source_target_pairs={{0,4},{1,5},{2,6},{3,7},{4,0},{5,1},{6,2},{7,3},{8,12},{9,13},{10,... | collective-permute-start | bytes 1572872 | tf_op jit(solution)/shard_map/ppermute | solution.py:284
  18.9 12.3 %collective-permute-start.10 = (bf16[256,1024]{1,0:T(8,128)(2,1)S(1)}, bf16[256,1024]{1,0:T(8,128)(2,1)S(1)}, u32[]{:S(2)}, u32[]{:S(2)}) collective-permute-start(bf16[256,1024]{1,0:T(8,128)(2,1)S(1)} %get-tuple-element.50), channel_id=1, source_target_pairs={{0,2},{1,3},{2,0},{3,1},{4,6},{5,7},{6,4},{7,5},{8,10},{9,11},{10,... | collective-permute-start | bytes 1572872 | tf_op jit(solution)/shard_map/ppermute | solution.py:284
  22.0 9.2 %collective-permute-start.11 = (bf16[256,1024]{1,0:T(8,128)(2,1)S(1)}, bf16[256,1024]{1,0:T(8,128)(2,1)S(1)}, u32[]{:S(2)}, u32[]{:S(2)}) collective-permute-start(bf16[256,1024]{1,0:T(8,128)(2,1)S(1)} %collective-permute-done.2.refs_0_), channel_id=1, source_target_pairs={{0,1},{1,0},{2,3},{3,2},{4,5},{5,4},{6,7},{7,6},{8,9},{9,8},{10,11... | collective-permute-start | bytes 1572872 | tf_op jit(solution)/shard_map/ppermute | solution.py:284
  22.0 10.8 %collective-permute-start.12 = (bf16[256,1024]{1,0:T(8,128)(2,1)S(1)}, bf16[256,1024]{1,0:T(8,128)(2,1)S(1)}, u32[]{:S(2)}, u32[]{:S(2)}) collective-permute-start(bf16[256,1024]{1,0:T(8,128)(2,1)S(1)} %collective-permute-done.3.refs_1_.refs_2_), channel_id=1, source_target_pairs={{0,1},{1,0},{2,3},{3,2},{4,5},{5,4},{6,7},{7,6},{8,9},{9,8},{10,11... | collective-permute-start | bytes 1572872 | tf_op jit(solution)/shard_map/ppermute | solution.py:284
  29.7 5.2 %collective-permute-start.14 = (bf16[256,1024]{1,0:T(8,128)(2,1)S(1)}, bf16[256,1024]{1,0:T(8,128)(2,1)S(1)}, u32[]{:S(2)}, u32[]{:S(2)}) collective-permute-start(bf16[256,1024]{1,0:T(8,128)(2,1)S(1)} %collective-permute-done.1.refs_3_.refs_1_), channel_id=1, source_target_pairs={{0,1},{1,0},{2,3},{3,2},{4,5},{5,4},{6,7},{7,6},{8,9},{9,8},{10,11... | collective-permute-start | bytes 1572872 | tf_op jit(solution)/shard_map/ppermute | solution.py:284
  29.7 6.7 %collective-permute-start.15 = (bf16[256,1024]{1,0:T(8,128)(2,1)S(1)}, bf16[256,1024]{1,0:T(8,128)(2,1)S(1)}, u32[]{:S(2)}, u32[]{:S(2)}) collective-permute-start(bf16[256,1024]{1,0:T(8,128)(2,1)S(1)} %collective-permute-done.4.refs_1_.refs_4_), channel_id=1, source_target_pairs={{0,1},{1,0},{2,3},{3,2},{4,5},{5,4},{6,7},{7,6},{8,9},{9,8},{10,11... | collective-permute-start | bytes 1572872 | tf_op jit(solution)/shard_map/ppermute | solution.py:284
  31.2 5.2 %collective-permute-start.13 = (bf16[256,1024]{1,0:T(8,128)(2,1)S(1)}, bf16[256,1024]{1,0:T(8,128)(2,1)S(1)}, u32[]{:S(2)}, u32[]{:S(2)}) collective-permute-start(bf16[256,1024]{1,0:T(8,128)(2,1)S(1)} %collective-permute-done.10.refs_2_), channel_id=1, source_target_pairs={{0,1},{1,0},{2,3},{3,2},{4,5},{5,4},{6,7},{7,6},{8,9},{9,8},{10,11... | collective-permute-start | bytes 1572872 | tf_op jit(solution)/shard_map/ppermute | solution.py:284
  31.2 14.3 %collective-permute-start.8 = (bf16[256,1024]{1,0:T(8,128)(2,1)S(1)}, bf16[256,1024]{1,0:T(8,128)(2,1)S(1)}, u32[]{:S(2)}, u32[]{:S(2)}) collective-permute-start(bf16[256,1024]{1,0:T(8,128)(2,1)S(1)} %get-tuple-element.68), channel_id=1, source_target_pairs={{0,4},{1,5},{2,6},{3,7},{4,0},{5,1},{6,2},{7,3},{8,12},{9,13},{10,... | collective-permute-start | bytes 1572872 | tf_op jit(solution)/shard_map/ppermute | solution.py:284
  32.8 14.0 %collective-permute-start.9 = (bf16[256,1024]{1,0:T(8,128)(2,1)S(1)}, bf16[256,1024]{1,0:T(8,128)(2,1)S(1)}, u32[]{:S(2)}, u32[]{:S(2)}) collective-permute-start(bf16[256,1024]{1,0:T(8,128)(2,1)S(1)} %get-tuple-element.69), channel_id=1, source_target_pairs={{0,8},{1,9},{2,10},{3,11},{4,12},{5,13},{6,14},{7,15},{8,16},{9,17... | collective-permute-start | bytes 1572872 | tf_op jit(solution)/shard_map/ppermute | solution.py:284
  34.9 13.7 %collective-permute-start.7 = (bf16[256,1024]{1,0:T(8,128)(2,1)S(1)}, bf16[256,1024]{1,0:T(8,128)(2,1)S(1)}, u32[]{:S(2)}, u32[]{:S(2)}) collective-permute-start(bf16[256,1024]{1,0:T(8,128)(2,1)S(1)} %collective-permute-done.1.refs_3_.refs_1_), channel_id=1, source_target_pairs={{0,2},{1,3},{2,0},{3,1},{4,6},{5,7},{6,4},{7,5},{8,10},{9,11},{10,... | collective-permute-start | bytes 1572872 | tf_op jit(solution)/shard_map/ppermute | solution.py:284
  36.4 17.4 %collective-permute-start.16 = (bf16[256,1024]{1,0:T(8,128)(2,1)S(1)}, bf16[256,1024]{1,0:T(8,128)(2,1)S(1)}, u32[]{:S(2)}, u32[]{:S(2)}) collective-permute-start(bf16[256,1024]{1,0:T(8,128)(2,1)S(1)} %collective-permute-done.refs_1_.refs_0_), channel_id=1, source_target_pairs={{0,1},{1,0},{2,3},{3,2},{4,5},{5,4},{6,7},{7,6},{8,9},{9,8},{10,11... | collective-permute-start | bytes 1572872 | tf_op jit(solution)/shard_map/ppermute | solution.py:284
  48.6 5.2 %collective-permute-start.17 = (bf16[256,1024]{1,0:T(8,128)(2,1)S(1)}, bf16[256,1024]{1,0:T(8,128)(2,1)S(1)}, u32[]{:S(2)}, u32[]{:S(2)}) collective-permute-start(bf16[256,1024]{1,0:T(8,128)(2,1)S(1)} %collective-permute-done.7.refs_2_), channel_id=1, source_target_pairs={{0,1},{1,0},{2,3},{3,2},{4,5},{5,4},{6,7},{7,6},{8,9},{9,8},{10,11... | collective-permute-start | bytes 1572872 | tf_op jit(solution)/shard_map/ppermute | solution.py:284
  48.6 5.2 %collective-permute-start.18 = (bf16[256,1024]{1,0:T(8,128)(2,1)S(1)}, bf16[256,1024]{1,0:T(8,128)(2,1)S(1)}, u32[]{:S(2)}, u32[]{:S(2)}) collective-permute-start(bf16[256,1024]{1,0:T(8,128)(2,1)S(1)} %collective-permute-done.8.refs_3_), channel_id=1, source_target_pairs={{0,1},{1,0},{2,3},{3,2},{4,5},{5,4},{6,7},{7,6},{8,9},{9,8},{10,11... | collective-permute-start | bytes 1572872 | tf_op jit(solution)/shard_map/ppermute | solution.py:284
  49.1 4.7 %collective-permute-start.19 = (bf16[256,1024]{1,0:T(8,128)(2,1)S(1)}, bf16[256,1024]{1,0:T(8,128)(2,1)S(1)}, u32[]{:S(2)}, u32[]{:S(2)}) collective-permute-start(bf16[256,1024]{1,0:T(8,128)(2,1)S(1)} %collective-permute-done.9.refs_4_), channel_id=1, source_target_pairs={{0,1},{1,0},{2,3},{3,2},{4,5},{5,4},{6,7},{7,6},{8,9},{9,8},{10,11... | collective-permute-start | bytes 1572872 | tf_op jit(solution)/shard_map/ppermute | solution.py:284
